TPU v7x, 128 devices: a whole 4x4x4 slice. The times are simulated.
128 devices in a mesh: expert: 16 (over x, y), tensor: 8 (over z, core).
Axes of the slice: x: 4, y: 4, z: 4, core: 2. Of those that a mesh axis runs over, the one named last changes fastest.
Arguments:
- layer_input: bfloat16 [16384, 1024], P(('expert', 'tensor')), may hold values from -6 to 6
- routes: int32 [16384, 8], P(('expert', 'tensor')), may hold values from 0 to 31, all different within a row; in each aligned block of 128 rows (0 to 127, 128 to 255, ...) at most 48 rows name the same one
- cotangent: bfloat16 [16384, 1024], P(('expert', 'tensor')), may hold values from -6 to 6
- gain_attn: float32 [1024], replicated, may hold values from 0.5 to 1.5
- gain_moe: float32 [1024], replicated, may hold values from 0.5 to 1.5
- w_query: bfloat16 [1024, 1024], P(None, 'tensor'), may hold values from -0.1875 to 0.1875
- w_key: bfloat16 [1024, 512], P(None, 'tensor'), may hold values from -0.1875 to 0.1875
- w_value: bfloat16 [1024, 512], P(None, 'tensor'), may hold values from -0.1875 to 0.1875
- w_out: bfloat16 [1024, 1024], P('tensor'), may hold values from -0.75 to 0.75
- w_router: bfloat16 [1024, 32], replicated, may hold values from -0.09375 to 0.09375
- w_gate: bfloat16 [32, 1024, 512], P('expert', None, 'tensor'), may hold values from -0.1875 to 0.1875
- w_up: bfloat16 [32, 1024, 512], P('expert', None, 'tensor'), may hold values from -0.1875 to 0.1875
- w_down: bfloat16 [32, 512, 1024], P('expert', 'tensor'), may hold values from -0.75 to 0.75
Outputs:
- output: bfloat16 [16384, 1024], P(('expert', 'tensor'))
- grad_input: float32 [16384, 1024], P(('expert', 'tensor'))
- grad_query: float32 [1024, 1024], P(None, 'tensor')
- grad_key: float32 [1024, 512], P(None, 'tensor')
- grad_value: float32 [1024, 512], P(None, 'tensor')
- grad_out: float32 [1024, 1024], P('tensor')
- grad_gain_attn: float32 [1024], replicated
- grad_gain_moe: float32 [1024], replicated
- grad_router: float32 [1024, 32], replicated
- grad_gate: float32 [32, 1024, 512], P('expert', None, 'tensor')
- grad_up: float32 [32, 1024, 512], P('expert', None, 'tensor')
- grad_down: float32 [32, 512, 1024], P('expert', 'tensor')
Inputs may be any that keep to these rules, and one draw needn't show every extreme that they name: `routes`: each row names 8 different experts. In each aligned block of 128 rows (the rows of one device) no expert is named by more than 48 rows, and in some block one expert is named by exactly 48 rows.
All inputs are finite; a program needn't handle non-finite values.
Results may differ from a plain program's by a relative error of at most 0.024.
Values may be sent and summed in bfloat16 or wider, within the bound.
A program may use at most 128 MiB of HBM per device.

v0:
```python
import jax
import jax.numpy as jnp
from jax import lax
from jax.sharding import Mesh
from jax.sharding import PartitionSpec as P

HEAD_DIM = 64
EXPERT = ("expert_0", "expert_1")
TENSOR = ("tensor_0", "tensor_1")
EXPERT_TENSOR = ("expert_0", "expert_1", "tensor_0", "tensor_1")


EPS = 1e-06
THETA = 10000.0
HIGH = lax.Precision.HIGHEST


def joined_along(tiles, dim):
    tiles = jnp.moveaxis(tiles, 0, dim)
    shape = tiles.shape
    return tiles.reshape(*shape[:dim], shape[dim] * shape[dim + 1], *shape[dim + 2 :])


def copy_for_each(shard, axis):
    copies = jnp.broadcast_to(shard, (lax.axis_size(axis), *shard.shape))
    return lax.all_to_all(copies, axis, split_axis=0, concat_axis=0, tiled=True)


def gathered_copies(shard, axis, dim):
    return joined_along(copy_for_each(shard, axis), dim)


def in_blocks(shard, dim, length):
    before, after = (shard.shape[:dim], shard.shape[dim + 1 :])
    return jnp.moveaxis(shard.reshape(*before, length, -1, *after), dim, 0)


def sent_and_summed(shard, axis, dim):
    tiles = in_blocks(shard, dim, lax.axis_size(axis))
    arrived = lax.all_to_all(tiles, axis, split_axis=0, concat_axis=0, tiled=True)
    return arrived.astype(jnp.float32).sum(axis=0)


def summed_rows(shard, axes, dim):
    far, near = axes
    tiles = in_blocks(shard, dim, lax.axis_size(far))
    nearer = sent_and_summed(tiles, near, dim + 1)
    arrived = lax.all_to_all(
        nearer.astype(jnp.bfloat16), far, split_axis=0, concat_axis=0, tiled=True
    )
    return arrived.astype(jnp.float32).sum(axis=0)


def gather_turned(arrays, axis, dims):
    turned = [jnp.moveaxis(a, dim, 0) for a, dim in zip(arrays, dims)]
    widths = [t[0].size for t in turned]
    both = jnp.concatenate([t.reshape(-1, w) for t, w in zip(turned, widths)], axis=1)
    whole = lax.all_gather(both, axis, axis=0, tiled=True)
    tiles = jnp.split(whole, [sum(widths[:k]) for k in range(1, len(widths))], axis=1)
    return tuple(
        (
            jnp.moveaxis(b.reshape(-1, *t.shape[1:]), 0, dim)
            for b, t, dim in zip(tiles, turned, dims)
        )
    )


def sent_together(arrays, axis, dim, along):
    both = jnp.concatenate(arrays, axis=along)
    whole, at, gathered = (lax.psum_scatter(both, axis, scatter_dimension=dim, tiled=True), 0, [])
    for a in arrays:
        gathered.append(lax.slice_in_dim(whole, at, at + a.shape[along], axis=along))
        at += a.shape[along]
    return tuple(gathered)


def rows_for(lines, length):
    spare = -len(lines) % length
    return jnp.pad(lines, [(0, spare)] + [(0, 0)] * (lines.ndim - 1))


def gathered_by_axis(shard, axes, dim):
    far, near = axes
    initial = copy_for_each(shard, far)
    tiles = jnp.swapaxes(copy_for_each(initial, near), 0, 1)
    return joined_along(tiles.reshape(-1, *shard.shape), dim)


def sum_at_owner(shard, axis, dim):
    length = lax.axis_size(axis)
    tiles = lax.all_to_all(in_blocks(shard, dim, length), axis, 0, 0, tiled=True)
    return jnp.sum(tiles, axis=0)


def summed_rows_2(shard, axes, dim):
    far, near = axes
    tiles = in_blocks(shard, dim, lax.axis_size(far))
    nearer = sum_at_owner(tiles, near, dim + 1)
    arrived = lax.all_to_all(nearer, far, split_axis=0, concat_axis=0, tiled=True)
    return arrived.sum(axis=0)


def total_of(shard, axes):
    padded = rows_for(shard, lax.axis_size(axes[0]) * lax.axis_size(axes[1]))
    whole = gathered_by_axis(summed_rows_2(padded, axes, 0), axes, 0)
    return lax.slice_in_dim(whole, 0, len(shard)).reshape(shard.shape)


def in_one(arrays, axis):
    ravelled, at, gathered = (jnp.concatenate([a.reshape(-1) for a in arrays]), 0, [])
    total = total_of(ravelled, axis)
    for a in arrays:
        gathered.append(total[at : at + a.size].reshape(a.shape))
        at += a.size
    return tuple(gathered)


def normalize(values, gain):
    inverse = lax.rsqrt(jnp.mean(values * values, -1, keepdims=True) + EPS)
    return (values * inverse * gain, inverse)


def norm_back(grad, values, inverse, gain):
    scaled = grad * gain
    normed = values * inverse
    inner = jnp.mean(scaled * normed, -1, keepdims=True)
    return (inverse * (scaled - normed * inner), jnp.sum(grad * normed, 0))


def rope_tables(length, width):
    half = width // 2
    freqs = THETA ** (-jnp.arange(half, dtype=jnp.float32) * 2.0 / width)
    angles = jnp.arange(length, dtype=jnp.float32)[:, None] * freqs[None, :]
    return (jnp.cos(angles)[:, None, :], jnp.sin(angles)[:, None, :])


def rotate(values, cosine, sine, sign):
    half = values.shape[-1] // 2
    first = values[..., :half]
    second = values[..., half:]
    return jnp.concatenate(
        [first * cosine - sign * second * sine, second * cosine + sign * first * sine], -1
    )


def block_scores(q_block, keys, start, scale):
    raw = jnp.einsum("qngd,knd->ngqk", q_block, keys, preferred_element_type=jnp.float32) * scale
    rows = start + jnp.arange(q_block.shape[0])
    causal = jnp.arange(keys.shape[0])[None, :] <= rows[:, None]
    return jnp.where(causal, raw, -1e30)


def attend_forward(query, keys, values, block_rows):
    length = query.shape[0]
    scale = query.shape[-1] ** (-0.5)

    def one(index):
        start = index * block_rows
        q_block = lax.dynamic_slice_in_dim(query, start, block_rows, 0)
        scores = block_scores(q_block, keys, start, scale)
        peak = jnp.max(scores, -1, keepdims=True)
        expo = jnp.exp(scores - peak)
        total = jnp.sum(expo, -1, keepdims=True)
        probs = (expo / total).astype(jnp.bfloat16)
        result = jnp.einsum("ngqk,knd->qngd", probs, values, preferred_element_type=jnp.float32)
        return (result, (peak + jnp.log(total))[..., 0])

    results, logsum = lax.map(one, jnp.arange(length // block_rows))
    return (results.reshape(length, -1), logsum)


def attend_backward(query, keys, values, grad_heads, logsum, block_rows):
    length = query.shape[0]
    scale = query.shape[-1] ** (-0.5)

    def one(carry, index):
        grad_keys, grad_values = carry
        start = index * block_rows
        q_block = lax.dynamic_slice_in_dim(query, start, block_rows, 0)
        d_block = lax.dynamic_slice_in_dim(grad_heads, start, block_rows, 0)
        scores = block_scores(q_block, keys, start, scale)
        probs = jnp.exp(scores - logsum[index][..., None])
        grad_probs = jnp.einsum(
            "qngd,knd->ngqk", d_block, values, preferred_element_type=jnp.float32
        )
        inner = jnp.sum(probs * grad_probs, -1, keepdims=True)
        grad_scores = (probs * (grad_probs - inner)).astype(jnp.bfloat16)
        grad_query = (
            jnp.einsum("ngqk,knd->qngd", grad_scores, keys, preferred_element_type=jnp.float32)
            * scale
        )
        grad_keys = (
            grad_keys
            + jnp.einsum("ngqk,qngd->knd", grad_scores, q_block, preferred_element_type=jnp.float32)
            * scale
        )
        grad_values = grad_values + jnp.einsum(
            "ngqk,qngd->knd",
            probs.astype(jnp.bfloat16),
            d_block,
            preferred_element_type=jnp.float32,
        )
        return ((grad_keys, grad_values), grad_query)

    empty = jnp.zeros(keys.shape, jnp.float32)
    (grad_keys, grad_values), grad_query = lax.scan(
        one, (empty, empty), jnp.arange(length // block_rows)
    )
    return (grad_query.reshape(query.shape), grad_keys, grad_values)


def to_owners(rows):
    return lax.all_to_all(rows, EXPERT, split_axis=0, concat_axis=0, tiled=True)


def per_device(
    layer_input,
    routes,
    cotangent,
    gain_attn,
    gain_moe,
    w_query,
    w_key,
    w_value,
    w_out,
    w_router,
    w_gate,
    w_up,
    w_down,
):
    tokens = layer_input.shape[0]
    width = layer_input.shape[1]
    top = routes.shape[1]
    groups = lax.axis_size(EXPERT)
    ranks = lax.axis_size(TENSOR)
    local = w_gate.shape[0]
    experts = local * groups
    capacity = max(2, 3 * tokens * top // (2 * experts))
    length = tokens * ranks
    block_rows = length // max(1, length // 512)
    heads_q = w_query.shape[1] // HEAD_DIM
    heads_kv = w_key.shape[1] // HEAD_DIM
    share = heads_q // heads_kv
    q_width = heads_q * HEAD_DIM
    kv_width = heads_kv * HEAD_DIM
    input_float = layer_input.astype(jnp.float32)
    normed, inverse_attn = normalize(input_float, gain_attn)
    normed_low = normed.astype(jnp.bfloat16)
    whole = gathered_copies(normed_low, TENSOR, 0)
    w_in = jnp.concatenate([w_query, w_key, w_value], 1)
    projected = jnp.dot(whole, w_in, preferred_element_type=jnp.float32)
    cosine, sine = rope_tables(length, HEAD_DIM)
    query = rotate(projected[:, :q_width].reshape(length, heads_q, HEAD_DIM), cosine, sine, 1.0)
    query = query.astype(jnp.bfloat16).reshape(length, heads_kv, share, HEAD_DIM)
    keys = rotate(
        projected[:, q_width : q_width + kv_width].reshape(length, heads_kv, HEAD_DIM),
        cosine,
        sine,
        1.0,
    ).astype(jnp.bfloat16)
    values = (
        projected[:, q_width + kv_width :].reshape(length, heads_kv, HEAD_DIM).astype(jnp.bfloat16)
    )
    heads_out, logsum = attend_forward(query, keys, values, block_rows)
    heads_low = heads_out.astype(jnp.bfloat16)
    attn = summed_rows(
        jnp.dot(heads_low, w_out, preferred_element_type=jnp.float32).astype(jnp.bfloat16),
        ("tensor_0", "tensor_1"),
        0,
    )
    hidden_in = input_float + attn
    mixed, inverse_moe = normalize(hidden_in, gain_moe)
    mixed_low = mixed.astype(jnp.bfloat16)
    logits = jnp.dot(mixed_low, w_router, preferred_element_type=jnp.float32)
    expert_iota = jnp.arange(experts, dtype=jnp.int32)
    choose = (routes[:, :, None] == expert_iota[None, None, :]).astype(jnp.float32)
    chosen = jnp.einsum("tke,te->tk", choose, logits, precision=HIGH)
    gates = jax.nn.softmax(chosen, axis=-1)
    flat = routes.reshape(-1)
    onehot = (flat[:, None] == expert_iota[None, :]).astype(jnp.int32)
    slot = jnp.sum(jnp.cumsum(onehot, 0) * onehot, 1) - 1
    cells = (flat // local * capacity + slot) * local + flat % local
    owner = jnp.arange(tokens * top) // top
    slots_all = groups * capacity * local
    send = jnp.zeros((slots_all, width), jnp.bfloat16).at[cells].set(mixed_low[owner])
    received = to_owners(send.reshape(groups * capacity, local, width))
    gate_all, up_all, down_all = gather_turned((w_gate, w_up, w_down), TENSOR, (2, 2, 1))
    gate_pre = jnp.einsum("red,edf->ref", received, gate_all, preferred_element_type=jnp.float32)
    up_pre = jnp.einsum("red,edf->ref", received, up_all, preferred_element_type=jnp.float32)
    hidden = (jax.nn.silu(gate_pre) * up_pre).astype(jnp.bfloat16)
    result = jnp.einsum(
        "ref,efd->red", hidden, down_all, preferred_element_type=jnp.float32
    ).astype(jnp.bfloat16)
    back = lax.all_to_all(result, EXPERT, split_axis=0, concat_axis=0, tiled=True)
    returned = back.reshape(slots_all, width)[cells].reshape(tokens, top, width).astype(jnp.float32)
    moe = jnp.einsum("tk,tkd->td", gates, returned, precision=HIGH)
    output = (hidden_in + moe).astype(jnp.bfloat16)
    grad_output = cotangent.astype(jnp.float32)
    grad_gates = jnp.einsum("tkd,td->tk", returned, grad_output, precision=HIGH)
    grad_returned = (
        (gates[:, :, None] * grad_output[:, None, :])
        .astype(jnp.bfloat16)
        .reshape(tokens * top, width)
    )
    grad_send = jnp.zeros((slots_all, width), jnp.bfloat16).at[cells].set(grad_returned)
    grad_received = to_owners(grad_send.reshape(groups * capacity, local, width))
    sigma = jax.nn.sigmoid(gate_pre)
    activation = gate_pre * sigma
    slope = sigma * (1.0 + gate_pre * (1.0 - sigma))
    grad_hidden = jnp.einsum(
        "red,efd->ref", grad_received, down_all, preferred_element_type=jnp.float32
    )
    down_full = jnp.einsum(
        "ref,red->efd", hidden, grad_received, preferred_element_type=jnp.float32
    )
    grad_gate_pre = (grad_hidden * up_pre * slope).astype(jnp.bfloat16)
    grad_up_pre = (grad_hidden * activation).astype(jnp.bfloat16)
    gate_full = jnp.einsum(
        "red,ref->edf", received, grad_gate_pre, preferred_element_type=jnp.float32
    )
    up_full = jnp.einsum("red,ref->edf", received, grad_up_pre, preferred_element_type=jnp.float32)
    grad_rows = jnp.einsum(
        "ref,edf->red", grad_gate_pre, gate_all, preferred_element_type=jnp.float32
    )
    grad_rows = grad_rows + jnp.einsum(
        "ref,edf->red", grad_up_pre, up_all, preferred_element_type=jnp.float32
    )
    grad_gate, grad_up, grad_down = (
        *tuple(
            (
                part.astype(jnp.float32)
                for part in sent_together(
                    (gate_full.astype(jnp.bfloat16), up_full.astype(jnp.bfloat16)), TENSOR, 2, 0
                )
            )
        ),
        lax.psum_scatter(
            down_full.astype(jnp.bfloat16), TENSOR, scatter_dimension=1, tiled=True
        ).astype(jnp.float32),
    )
    grad_back = lax.all_to_all(
        grad_rows.astype(jnp.bfloat16), EXPERT, split_axis=0, concat_axis=0, tiled=True
    ).astype(grad_rows.dtype)
    grad_mixed = jnp.sum(grad_back.reshape(slots_all, width)[cells].reshape(tokens, top, width), 1)
    inner_gates = jnp.sum(gates * grad_gates, -1, keepdims=True)
    grad_chosen = gates * (grad_gates - inner_gates)
    grad_logits = jnp.einsum("tke,tk->te", choose, grad_chosen, precision=HIGH)
    grad_router = jnp.einsum(
        "td,te->de", mixed_low.astype(jnp.float32), grad_logits, precision=HIGH
    )
    grad_mixed = grad_mixed + jnp.einsum(
        "te,de->td", grad_logits, w_router.astype(jnp.float32), precision=HIGH
    )
    grad_hidden_in, grad_gain_moe = norm_back(grad_mixed, hidden_in, inverse_moe, gain_moe)
    grad_hidden_in = grad_hidden_in + grad_output
    grad_attn_all = gathered_copies(grad_hidden_in.astype(jnp.bfloat16), TENSOR, 0)
    grad_heads = jnp.einsum(
        "sd,cd->sc", grad_attn_all, w_out, preferred_element_type=jnp.float32
    ).astype(jnp.bfloat16)
    grad_w_out = jnp.einsum(
        "sc,sd->cd", heads_low, grad_attn_all, preferred_element_type=jnp.float32
    )
    grad_q, grad_k, grad_v = attend_backward(
        query,
        keys,
        values,
        grad_heads.reshape(length, heads_kv, share, HEAD_DIM),
        logsum,
        block_rows,
    )
    grad_q = rotate(grad_q.reshape(length, heads_q, HEAD_DIM), cosine, sine, -1.0)
    grad_k = rotate(grad_k, cosine, sine, -1.0)
    grad_proj = jnp.concatenate(
        [
            grad_q.reshape(length, q_width),
            grad_k.reshape(length, kv_width),
            grad_v.reshape(length, kv_width),
        ],
        1,
    ).astype(jnp.bfloat16)
    grad_w_in = jnp.einsum("sd,sc->dc", whole, grad_proj, preferred_element_type=jnp.float32)
    part = grad_proj
    grad_normed = summed_rows(
        jnp.einsum("sc,dc->sd", part, w_in, preferred_element_type=jnp.float32).astype(
            jnp.bfloat16
        ),
        ("tensor_0", "tensor_1"),
        0,
    )
    grad_input, grad_gain_attn = norm_back(grad_normed, input_float, inverse_attn, gain_attn)
    grad_input = grad_input + grad_hidden_in
    sum_query, sum_key, sum_value, sum_out = (
        lax.psum(grad_w_in[:, :q_width].astype(jnp.bfloat16), EXPERT).astype(jnp.float32),
        lax.psum(grad_w_in[:, q_width : q_width + kv_width].astype(jnp.bfloat16), EXPERT).astype(
            jnp.float32
        ),
        lax.psum(grad_w_in[:, q_width + kv_width :].astype(jnp.bfloat16), EXPERT).astype(
            jnp.float32
        ),
        lax.psum(grad_w_out.astype(jnp.bfloat16), EXPERT).astype(jnp.float32),
    )
    sum_gain_attn, sum_gain_moe, sum_router = in_one(
        (grad_gain_attn, grad_gain_moe, grad_router),
        (("expert_0", "expert_1", "tensor_0"), "tensor_1"),
    )
    return (
        output,
        grad_input,
        sum_query,
        sum_key,
        sum_value,
        sum_out,
        sum_gain_attn,
        sum_gain_moe,
        sum_router,
        grad_gate,
        grad_up,
        grad_down,
    )


def solution(mesh):
    split = Mesh(mesh.devices.reshape(4, 4, 4, 2), ("expert_0", "expert_1", "tensor_0", "tensor_1"))
    in_specs = (
        P(EXPERT_TENSOR, None),
        P(EXPERT_TENSOR, None),
        P(EXPERT_TENSOR, None),
        P(),
        P(),
        P(None, TENSOR),
        P(None, TENSOR),
        P(None, TENSOR),
        P(TENSOR, None),
        P(),
        P(EXPERT, None, TENSOR),
        P(EXPERT, None, TENSOR),
        P(EXPERT, TENSOR, None),
    )
    out_specs = (
        P(EXPERT_TENSOR, None),
        P(EXPERT_TENSOR, None),
        P(None, TENSOR),
        P(None, TENSOR),
        P(None, TENSOR),
        P(TENSOR, None),
        P(),
        P(),
        P(),
        P(EXPERT, None, TENSOR),
        P(EXPERT, None, TENSOR),
        P(EXPERT, TENSOR, None),
    )
    return jax.shard_map(
        per_device, mesh=split, in_specs=in_specs, out_specs=out_specs, check_vma=False
    )
```

profile of v0, /device:TPU:1, one launch (start us, length us, event | category | flops | bytes accessed | tf_op | source)
XLA Modules:
  0.0 641.7 jit_solution(2870634254593937726)
XLA Ops:
  11.5 6.9 %all-to-all-start = ((bf16[8,128,1024]{2,1,0:T(8,128)(2,1)}), bf16[8,128,1024]{2,1,0:T(8,128)(2,1)S(1)}, u32[]{:S(2)}, u32[]{:S(2)}) async-start(bf16[8,128,1024]{2,1,0:T(8,128)(2,1)} %broadcast_in_dim.40), calls=%async_computation | async-start | bytes 4194304 | tf_op jit(solution)/shard_map/all_to_all | solution.py:26
  19.9 9.0 %reduce-window.6 = s32[32,8,128]{2,1,0:T(8,128)S(1)} reduce-window(s32[32,8,128]{2,1,0:T(8,128)S(1)} %fusion.118, s32[]{:T(128)} %constant.114.clone.1), window={size=1x1x128 pad=0_0x0_0x127_0}, to_apply=%region_10.11 | reduce-window | flops 4161536 | bytes 262148 | tf_op jit(solution)/shard_map/reduce-window
  31.7 21.0 %all-to-all-done = bf16[8,128,1024]{2,1,0:T(8,128)(2,1)S(1)} async-done(((bf16[8,128,1024]{2,1,0:T(8,128)(2,1)}), bf16[8,128,1024]{2,1,0:T(8,128)(2,1)S(1)}, u32[]{:S(2)}, u32[]{:S(2)}) %all-to-all-start) | async-done | bytes 2097184 | tf_op jit(solution)/shard_map/all_to_all | solution.py:26
  56.3 13.9 %while.27 = (s32[]{:T(128)}, bf16[2,512,1,2,64]{1,4,3,2,0:T(8,128)(2,1)}, f32[2,1,2,512]{3,2,1,0:T(2,128)S(1)}, s32[2]{0:T(128)S(1)}, bf16[1024,1,2,64]{0,3,2,1:...) while((s32[]{:T(128)}, ...), condition=%wide.region_4.5_spmd, body=%wide.region_1.4_spmd.sunk | while | flops 281542144 | bytes 17469688 | solution.py:168
  72.5 6.9 %all_to_all.78 = bf16[2,4,128,1024]{3,2,1,0:T(8,128)(2,1)S(1)} all-to-all(bf16[2,4,128,1024]{3,2,1,0:T(8,128)(2,1)S(1)} %bitcast.419), channel_id=1, replica_groups=mesh['expert_0'=4,'expert_1'=4,'tensor_0'=4,'tensor_1'=2] {'tensor_1'}, dimensions={0} | all-to-all | bytes 4194304 | tf_op jit(solution)/shard_map/all_to_all | solution.py:40
  85.8 14.0 %all-to-all-done.2 = bf16[4,128,1024]{2,1,0:T(8,128)(2,1)S(1)} async-done(((bf16[4,128,1024]{2,1,0:T(8,128)(2,1)}), bf16[4,128,1024]{2,1,0:T(8,128)(2,1)S(1)}, u32[]{:S(2)}, u32[]{:S(2)}) %all-to-all-start.2) | async-done | bytes 1048608 | tf_op jit(solution)/shard_map/all_to_all | solution.py:48
  101.8 16.4 %scatter_custom_fusion = bf16[1536,1024]{1,0:T(8,128)(2,1)S(1)} fusion(s32[1024]{0:T(1024)S(1)} %bitcast.454, bf16[128,1024]{1,0:T(8,128)(2,1)} %multiply_convert_fusion, s32[1024]{0:T(1024)} %broadcast_clamp_fusion.1, bf16[]{:T(256)} %constant.120.clone.1), kind=kCustom, calls=%fused_computation.105 | custom fusion | bytes 3146240 | tf_op jit(solution)/shard_map/scatter | solution.py:285
  121.4 44.2 %all_to_all.79 = bf16[768,2,1024]{2,1,0:T(2,128)(2,1)S(1)} all-to-all(bf16[768,2,1024]{2,1,0:T(2,128)(2,1)} %reshape.571), channel_id=1, replica_groups=mesh['expert_0'=4,'expert_1'=4,'tensor_0'=4,'tensor_1'=2] {'expert_0','e..., dimensions={0} | all-to-all | bytes 6291456 | tf_op jit(solution)/shard_map/all_to_all | solution.py:213
  165.6 6.2 copy.202
  171.8 5.9 fusion.128
  204.0 5.9 copy.188
  218.3 32.6 %all-to-all-done.4 = bf16[768,2,1024]{2,1,0:T(2,128)(2,1)} async-done(((bf16[768,2,1024]{2,1,0:T(2,128)(2,1)}), bf16[768,2,1024]{2,1,0:T(2,128)(2,1)}, u32[]{:S(2)}, u32[]{:S(2)}) %all-to-all-start.4) | async-done | bytes 3145760 | tf_op jit(solution)/shard_map/all_to_all | solution.py:294
  265.2 7.4 %scatter_custom_fusion.1 = bf16[1536,1024]{1,0:T(8,128)(2,1)S(1)} fusion(s32[1024]{0:T(1024)} %bitcast.455, f32[128,1024]{1,0:T(8,128)} %convert_element_type.159, f32[1024]{0:T(1024)} %mul.485, bf16[]{:T(256)} %constant.120.clone.1), kind=kCustom, calls=%fused_computation.94 | custom fusion | flops 2097152 | bytes 3674624 | tf_op jit(solution)/shard_map/scatter | solution.py:305
  275.9 42.5 %all_to_all.80 = bf16[768,2,1024]{2,1,0:T(2,128)(2,1)S(1)} all-to-all(bf16[768,2,1024]{2,1,0:T(2,128)(2,1)} %reshape.575), channel_id=1, replica_groups=mesh['expert_0'=4,'expert_1'=4,'tensor_0'=4,'tensor_1'=2] {'expert_0','e..., dimensions={0} | all-to-all | bytes 6291456 | tf_op jit(solution)/shard_map/all_to_all | solution.py:213
  318.4 6.0 fusion.62
  330.5 8.0 %copy.206 = bf16[4,1024,512]{1,0,2:T(4,128)(2,1)} copy(bf16[4,1024,512]{2,1,0:T(8,128)(2,1)} %pad_maximum_fusion) | data formatting | bytes 8388608 | tf_op jit(solution)/shard_map/concatenate | solution.py:69
  345.3 6.0 copy.195
  351.2 6.9 %all-to-all-start.6 = ((bf16[768,2,1024]{2,1,0:T(2,128)(2,1)}), bf16[768,2,1024]{2,1,0:T(2,128)(2,1)S(1)}, u32[]{:S(2)}, u32[]{:S(2)}) async-start(bf16[768,2,1024]{2,1,0:T(2,128)(2,1)} %copy.195), calls=%async_computation.6 | async-start | bytes 6291456 | tf_op jit(solution)/shard_map/all_to_all | solution.py:341
  358.1 5.7 fusion.87
  366.9 26.5 %all-to-all-done.6 = bf16[768,2,1024]{2,1,0:T(2,128)(2,1)S(1)} async-done(((bf16[768,2,1024]{2,1,0:T(2,128)(2,1)}), bf16[768,2,1024]{2,1,0:T(2,128)(2,1)S(1)}, u32[]{:S(2)}, u32[]{:S(2)}) %all-to-all-start.6) | async-done | bytes 3145760 | tf_op jit(solution)/shard_map/all_to_all | solution.py:341
  397.1 9.3 %gather_fusion.1 = f32[1024,1024]{1,0:T(8,128)} fusion(f32[1536,1024]{1,0:T(8,128)} %reshape.586, s32[1024]{0:T(1024)S(1)} %broadcast_clamp_fusion), kind=kCustom, calls=%fused_computation.2 | custom fusion | bytes 8392704 | tf_op jit(solution)/shard_map/gather | solution.py:344
  413.1 11.1 %all-to-all-start.7 = ((bf16[8,128,1024]{2,1,0:T(8,128)(2,1)}), bf16[8,128,1024]{2,1,0:T(8,128)(2,1)S(1)}, u32[]{:S(2)}, u32[]{:S(2)}) async-start(bf16[8,128,1024]{2,1,0:T(8,128)(2,1)} %broadcast_in_dim.42), calls=%async_computation.7 | async-start | bytes 4194304 | tf_op jit(solution)/shard_map/all_to_all | solution.py:26
  436.4 21.7 %reduce-scatter.2.cloned.1.call-done = bf16[2,64,1024]{2,1,0:T(8,128)(2,1)} async-done(((bf16[2,512,1024]{2,1,0:T(8,128)(2,1)}), bf16[2,64,1024]{2,1,0:T(8,128)(2,1)}) %reduce-scatter.2.cloned.1.call-update) | async-done | bytes 262160 | tf_op jit(solution)/shard_map/reduce_scatter | solution.py:337
  462.3 40.6 %while.28 = (s32[]{:T(128)}, f32[1024,1,64]{0,2,1:T(8,128)}, f32[1024,1,64]{0,2,1:T(8,128)}, f32[2,512,1,2,64]{1,0,4,3,2:T(2,128)}, s32[2]{0:T(128)}, /*index=5*...) while((s32[]{:T(128)}, f32[1024,1,64]{0,2,1:T(8,128)}, ...), condition=%wide.region_20.21_spmd.clone, body=%wide.region_18.20_spmd.clone.sunk | while | flops 687734272 | bytes 36864276 | solution.py:206
  476.3 5.8 dynamic_update_slice.19
  497.2 5.8 dynamic_update_slice.19
  511.3 10.5 %all_to_all.81 = bf16[2,4,128,1024]{3,2,1,0:T(8,128)(2,1)} all-to-all(bf16[2,4,128,1024]{3,2,1,0:T(8,128)(2,1)S(1)} %bitcast.420), channel_id=1, replica_groups=mesh['expert_0'=4,'expert_1'=4,'tensor_0'=4,'tensor_1'=2] {'tensor_1'}, dimensions={0} | all-to-all | bytes 4194304 | tf_op jit(solution)/shard_map/all_to_all | solution.py:40
  534.6 9.7 %all-to-all-done.9 = bf16[4,128,1024]{2,1,0:T(8,128)(2,1)} async-done(((bf16[4,128,1024]{2,1,0:T(8,128)(2,1)}), bf16[4,128,1024]{2,1,0:T(8,128)(2,1)}, u32[]{:S(2)}, u32[]{:S(2)}) %all-to-all-start.9) | async-done | bytes 1048608 | tf_op jit(solution)/shard_map/all_to_all | solution.py:48
  552.4 7.0 %all-to-all-start.11 = ((f32[64,1,272]{2,1,0:T(1,128)}), f32[64,1,272]{2,1,0:T(1,128)S(1)}, u32[]{:S(2)}, u32[]{:S(2)}) async-start(f32[64,1,272]{2,1,0:T(1,128)} %all_to_all.59), calls=%async_computation.11 | async-start | bytes 196608 | tf_op jit(solution)/shard_map/all_to_all | solution.py:99
  559.4 8.5 %all-to-all-done.11 = f32[64,1,272]{2,1,0:T(1,128)S(1)} async-done(((f32[64,1,272]{2,1,0:T(1,128)}), f32[64,1,272]{2,1,0:T(1,128)S(1)}, u32[]{:S(2)}, u32[]{:S(2)}) %all-to-all-start.11) | async-done | bytes 69664 | tf_op jit(solution)/shard_map/all_to_all | solution.py:99
  575.0 44.8 %all-reduce.7.cloned.1.call-done = (bf16[1024,128]{0,1:T(8,128)(2,1)}, bf16[1024,64]{0,1:T(8,128)(2,1)}, bf16[1024,64]{0,1:T(8,128)(2,1)}, bf16[128,1024]{1,0:T(8,128)(2,1)}) async-done(((bf16[1024,128]{0,1:T(8,128)(2,1)}, bf16[1024,64]{0,1:T(8,128)(2,1)}, bf16[1024,64]{0,1:T(8,128)(2,1)}, bf16[128,1024]{1,0:T(8,128)(2,1)}), (bf16[1024,128]{0,1:T(8,128)(2,1)}, bf16[1024,64]{0,1:T(8,128)(2,1)}, ...) | async-done | bytes 786448 | tf_op jit(solution)/shard_map/psum | solution.py:393
  626.8 5.6 all_to_all.83
  (338 shorter events, 201.4 us)
Async XLA Ops:
  7.2 64.4 %copy-start = (bf16[128,1024]{1,0:T(8,128)(2,1)S(1)}, bf16[128,1024]{1,0:T(8,128)(2,1)}, u32[]{:S(2)}) copy-start(bf16[128,1024]{1,0:T(8,128)(2,1)} %param.25) | copy-start | bytes 786436
  11.5 41.1 %all-to-all-start = ((bf16[8,128,1024]{2,1,0:T(8,128)(2,1)}), bf16[8,128,1024]{2,1,0:T(8,128)(2,1)S(1)}, u32[]{:S(2)}, u32[]{:S(2)}) async-start(bf16[8,128,1024]{2,1,0:T(8,128)(2,1)} %broadcast_in_dim.40), calls=%async_computation | async-start | bytes 4194304 | tf_op jit(solution)/shard_map/all_to_all | solution.py:26
  18.5 153.3 %all-gather.2.cloned.1.call-start = ((), (), s32[]{:S(2)}) async-start(), calls=%async_computation.15 | async-start | bytes 7077888 | tf_op jit(solution)/shard_map/all_gather | solution.py:58
  19.7 65.3 %copy-start.31 = (s32[128,8]{1,0:T(8,128)}, s32[128,8]{1,0:T(8,128)S(1)}, u32[]{:S(2)}) copy-start(s32[128,8]{1,0:T(8,128)S(1)} %copy.171) | copy-start | bytes 12292
  29.5 23.2 %copy-start.39 = (bf16[1024,64]{1,0:T(8,128)(2,1)}, bf16[1024,64]{1,0:T(8,128)(2,1)S(1)}, u32[]{:S(2)}) copy-start(bf16[1024,64]{1,0:T(8,128)(2,1)S(1)} %copy.167) | copy-start | bytes 393220
  30.5 25.0 %copy-start.64 = (f32[32]{0:T(128)}, f32[32]{0:T(128)S(1)}, u32[]{:S(2)}) copy-start(f32[32]{0:T(128)S(1)} %multiply_power_fusion) | copy-start | bytes 388
  31.7 23.9 %copy-start.30 = (f32[1024,32]{0,1:T(8,128)}, f32[1024,32]{0,1:T(8,128)S(1)}, u32[]{:S(2)}) copy-start(f32[1024,32]{0,1:T(8,128)S(1)} %get-tuple-element.275) | copy-start | bytes 393220
  79.4 20.6 %copy-start.8 = (bf16[128,1024]{1,0:T(8,128)(2,1)S(1)}, bf16[128,1024]{1,0:T(8,128)(2,1)}, u32[]{:S(2)}) copy-start(bf16[128,1024]{1,0:T(8,128)(2,1)} %param.17) | copy-start | bytes 786436
  81.1 19.8 %copy-start.55 = (f32[1024]{0:T(1024)S(1)}, f32[1024]{0:T(1024)}, u32[]{:S(2)}) copy-start(f32[1024]{0:T(1024)} %param.21) | copy-start | bytes 12292
  81.1 18.7 %all-to-all-start.2 = ((bf16[4,128,1024]{2,1,0:T(8,128)(2,1)}), bf16[4,128,1024]{2,1,0:T(8,128)(2,1)S(1)}, u32[]{:S(2)}, u32[]{:S(2)}) async-start(bf16[4,128,1024]{2,1,0:T(8,128)(2,1)} %reduce_sum.169), calls=%async_computation.2 | async-start | bytes 2097152 | tf_op jit(solution)/shard_map/all_to_all | solution.py:48
  85.8 32.4 %copy-start.57 = (s32[1024,1]{0,1:T(1,128)}, s32[1024,1]{0,1:T(1,128)S(1)}, u32[]{:S(2)}) copy-start(s32[1024,1]{0,1:T(1,128)S(1)} %compare_select_fusion.1) | copy-start | bytes 12292
  209.9 41.0 %all-to-all-start.4 = ((bf16[768,2,1024]{2,1,0:T(2,128)(2,1)}), bf16[768,2,1024]{2,1,0:T(2,128)(2,1)}, u32[]{:S(2)}, u32[]{:S(2)}) async-start(bf16[768,2,1024]{2,1,0:T(2,128)(2,1)} %copy.188), calls=%async_computation.4 | async-start | bytes 6291456 | tf_op jit(solution)/shard_map/all_to_all | solution.py:294
  215.3 217.6 %all-reduce.5.cloned.1.call-start = ((), (), s32[]{:S(2)}) async-start(), calls=%async_computation.17 | async-start | bytes 8388608
  275.9 42.5 %copy-start.24 = (bf16[512,2048]{0,1:T(8,128)(2,1)S(1)}, bf16[512,2048]{0,1:T(8,128)(2,1)}, u32[]{:S(2)}) copy-start(bf16[512,2048]{0,1:T(8,128)(2,1)} %copy.175) | copy-start | bytes 6291460
  275.9 42.5 %copy-start.73 = (f32[2,512,768]{2,1,0:T(8,128)S(1)}, f32[2,512,768]{2,1,0:T(8,128)}, u32[]{:S(2)}) copy-start(f32[2,512,768]{2,1,0:T(8,128)} %copy-done.72) | copy-start | bytes 9437188
  351.2 42.1 %all-to-all-start.6 = ((bf16[768,2,1024]{2,1,0:T(2,128)(2,1)}), bf16[768,2,1024]{2,1,0:T(2,128)(2,1)S(1)}, u32[]{:S(2)}, u32[]{:S(2)}) async-start(bf16[768,2,1024]{2,1,0:T(2,128)(2,1)} %copy.195), calls=%async_computation.6 | async-start | bytes 6291456 | tf_op jit(solution)/shard_map/all_to_all | solution.py:341
  358.1 100.0 %reduce-scatter.2.cloned.1.call-start = ((), (), s32[]{:S(2)}) async-start(), calls=%async_computation.16 | async-start | bytes 2359296 | tf_op jit(solution)/shard_map/reduce_scatter | solution.py:337
  411.5 14.0 %copy-start.21 = (bf16[128,1024]{1,0:T(8,128)(2,1)S(1)}, bf16[128,1024]{1,0:T(8,128)(2,1)}, u32[]{:S(2)}) copy-start(bf16[128,1024]{1,0:T(8,128)(2,1)} %multiply_convert_fusion) | copy-start | bytes 786436
  411.5 14.0 %copy-start.51 = (f32[128,1,32]{2,1,0:T(1,128)S(1)}, f32[128,1,32]{2,1,0:T(1,128)}, u32[]{:S(2)}) copy-start(f32[128,1,32]{2,1,0:T(1,128)} %fusion.105) | copy-start | bytes 49156
  413.1 15.5 %copy-start.34 = (f32[128,8]{1,0:T(8,128)S(1)}, f32[128,8]{1,0:T(8,128)}, u32[]{:S(2)}) copy-start(f32[128,8]{1,0:T(8,128)} %copy-done.33) | copy-start | bytes 12292
  413.1 47.2 %all-to-all-start.7 = ((bf16[8,128,1024]{2,1,0:T(8,128)(2,1)}), bf16[8,128,1024]{2,1,0:T(8,128)(2,1)S(1)}, u32[]{:S(2)}, u32[]{:S(2)}) async-start(bf16[8,128,1024]{2,1,0:T(8,128)(2,1)} %broadcast_in_dim.42), calls=%async_computation.7 | async-start | bytes 4194304 | tf_op jit(solution)/shard_map/all_to_all | solution.py:26
  434.5 27.9 %copy-start.7 = (bf16[1024,1,2,64]{0,3,2,1:T(8,128)(2,1)S(1)}, bf16[1024,1,2,64]{0,3,2,1:T(8,128)(2,1)}, u32[]{:S(2)}) copy-start(bf16[1024,1,2,64]{0,3,2,1:T(8,128)(2,1)} %copy-done.6) | copy-start | bytes 786436
  525.2 19.2 %all-to-all-start.9 = ((bf16[4,128,1024]{2,1,0:T(8,128)(2,1)}), bf16[4,128,1024]{2,1,0:T(8,128)(2,1)}, u32[]{:S(2)}, u32[]{:S(2)}) async-start(bf16[4,128,1024]{2,1,0:T(8,128)(2,1)} %reduce_sum.177), calls=%async_computation.9 | async-start | bytes 2097152 | tf_op jit(solution)/shard_map/all_to_all | solution.py:48
  529.4 90.4 %all-reduce.7.cloned.1.call-start = ((), (), s32[]{:S(2)}) async-start(), calls=%async_computation.18 | async-start | bytes 1572864 | tf_op jit(solution)/shard_map/psum | solution.py:393
  534.5 39.3 %copy-start.11 = (f32[128,1024]{1,0:T(8,128)S(1)}, f32[128,1024]{1,0:T(8,128)}, u32[]{:S(2)}) copy-start(f32[128,1024]{1,0:T(8,128)} %copy-done.10) | copy-start | bytes 1572868
  534.5 39.3 %copy-start.19 = (bf16[128,1024]{1,0:T(8,128)(2,1)S(1)}, bf16[128,1024]{1,0:T(8,128)(2,1)}, u32[]{:S(2)}) copy-start(bf16[128,1024]{1,0:T(8,128)(2,1)} %param.19) | copy-start | bytes 786436
  534.5 39.3 %copy-start.26 = (f32[128,1,1024]{2,1,0:T(1,128)S(1)}, f32[128,1,1024]{2,1,0:T(1,128)}, u32[]{:S(2)}) copy-start(f32[128,1,1024]{2,1,0:T(1,128)} %fusion.77) | copy-start | bytes 1572868
  534.5 39.3 %copy-start.61 = (f32[128]{0:T(128)S(1)}, f32[128]{0:T(128)}, u32[]{:S(2)}) copy-start(f32[128]{0:T(128)} %copy-done.59) | copy-start | bytes 1540
  534.5 39.3 %copy-start.63 = (f32[128]{0:T(128)S(1)}, f32[128]{0:T(128)}, u32[]{:S(2)}) copy-start(f32[128]{0:T(128)} %copy-done.62) | copy-start | bytes 1540
  534.5 39.3 %copy-start.69 = (f32[128]{0:T(128)S(1)}, f32[128]{0:T(128)}, u32[]{:S(2)}) copy-start(f32[128]{0:T(128)} %copy-done.68) | copy-start | bytes 1540
  552.4 15.5 %all-to-all-start.11 = ((f32[64,1,272]{2,1,0:T(1,128)}), f32[64,1,272]{2,1,0:T(1,128)S(1)}, u32[]{:S(2)}, u32[]{:S(2)}) async-start(f32[64,1,272]{2,1,0:T(1,128)} %all_to_all.59), calls=%async_computation.11 | async-start | bytes 196608 | tf_op jit(solution)/shard_map/all_to_all | solution.py:99
  568.7 58.0 %all-to-all-start.12 = ((f32[64,1,272]{2,1,0:T(1,128)}), f32[64,1,272]{2,1,0:T(1,128)S(1)}, u32[]{:S(2)}, u32[]{:S(2)}) async-start(f32[64,1,272]{2,1,0:T(1,128)} %broadcast_in_dim.43), calls=%async_computation.12 | async-start | bytes 196608 | tf_op jit(solution)/shard_map/all_to_all | solution.py:26
  (57 other events, 256.1 us)
Sparse Core Ops, SparseCore 0:
  21.0 51.1 all-gather.1
  338.6 73.2 all-reduce.4
  414.3 43.6 reduce-scatter.1
  534.7 85.0 all-reduce.6
where the time goes:
time: 651 us; the launch traced here: 642 us
  waiting for transfers between devices  179 us (27%)
  local copies, waits for them, and re-layouts  139 us (21%)
  blocking collectives  114 us (18%)
  matrix products  75.4 us (12%)
  other arithmetic  60 us (9%)
  starting transfers between devices  51 us (8%)
  between operations  16.1 us (2%)
  loops' own time  6.68 us (1%)
    all_to_all x2, blocking collectives, to_owners(): return lax.all_to_all(rows, EXPERT, split_axis=0, concat_axis=0, tiled=True)  86.7 us
    psum x1, waiting for transfers between devices, per_device(): lax.psum(grad_w_in[:, :q_width].astype(jnp.bfloat16), EXPERT)  44.8 us
    all_to_all x1, waiting for transfers between devices, per_device(): lax.all_to_all(result, EXPERT, split_axis=0, concat_axis=0, tiled=True)  32.6 us
    all_to_all x1, waiting for transfers between devices, per_device(): lax.all_to_all(grad_rows.astype(jnp.bfloat16), EXPERT, split_axis=0, conc...  26.5 us
    all_to_all x2, waiting for transfers between devices, summed_rows(): lax.all_to_all(nearer.astype(jnp.bfloat16), far, split_axis=0, concat_axi...  23.7 us
    all_to_all x3, starting transfers between devices, copy_for_each(): return lax.all_to_all(copies, axis, split_axis=0, concat_axis=0, tiled=True)  23.1 us
    reduce_scatter x1, waiting for transfers between devices, per_device(): lax.psum_scatter(down_full.astype(jnp.bfloat16), TENSOR, scatter_dimensio...  21.7 us
    all_to_all x3, waiting for transfers between devices, copy_for_each(): return lax.all_to_all(copies, axis, split_axis=0, concat_axis=0, tiled=True)  21.4 us
  transfers between devices with their start and end apart: 12, of which 9 were waited for; matrix products, arithmetic and copies ran while one was open for 20% of the time, Pallas kernels for 0%

commit v1 on v0

v1 whole, which is shorter than its diff:
```python
import functools

import jax
import jax.numpy as jnp
import numpy as np
from jax import lax
from jax.experimental import pallas as pl
from jax.experimental.pallas import tpu as pltpu
from jax.sharding import Mesh
from jax.sharding import PartitionSpec as P

AXES = ("expert_0", "expert_1", "tensor_0", "tensor_1")
EXPERT = ("expert_0", "expert_1")
TENSOR = ("tensor_0", "tensor_1")
MESH = pl.DeviceIdType.MESH
EPS = 1e-06
THETA = 10000.0
F32 = jnp.float32
BF16 = jnp.bfloat16
ROWS = 128
WIDTH = 1024
SEQ = 1024
HEAD = 64
CAP = 48
HALF = 64
NN = (((1,), (0,)), ((), ()))
NT = (((1,), (1,)), ((), ()))
TN = (((0,), (0,)), ((), ()))


def mul(a, b, dims=NN):
    return lax.dot_general(a, b, dims, preferred_element_type=F32)


def place():
    return tuple(lax.axis_index(a) for a in AXES)


def wrap(v):
    return lax.rem(v, 4)


def send(src, dst, out, arrive, device):
    return pltpu.make_async_remote_copy(
        src_ref=src, dst_ref=dst, send_sem=out, recv_sem=arrive, device_id=device, device_id_type=MESH
    )


def greet(devices):
    barrier = pltpu.get_barrier_semaphore()
    for device in devices:
        pl.semaphore_signal(barrier, inc=1, device_id=device, device_id_type=MESH)
    pl.semaphore_wait(barrier, len(devices))


def z_peers(me):
    x, y, z, c = me
    return [(x, y, wrap(z + d), c) for d in (1, 2, 3)] + [(x, y, z, 1 - c)]


def line_peers(me):
    x, y, z, c = me
    return [(wrap(x + d), y, z, c) for d in (1, 2, 3)] + [(x, wrap(y + d), z, c) for d in (1, 2, 3)]


class TensorGather:
    def __init__(self, me, slot, out, arrive):
        self.me, self.slot, self.out, self.arrive = me, slot, out, arrive

    def copy(self, k, source_z, source_c, device):
        ref = self.slot(source_z * 2 + source_c)
        return send(ref, ref, self.out.at[k], self.arrive.at[k], device)

    def start(self):
        x, y, z, c = self.me
        for d in (1, 3, 2):
            self.copy(d - 1, z, c, (x, y, wrap(z + d), c)).start()
        self.copy(3, z, c, (x, y, z, 1 - c)).start()

    def forward(self):
        x, y, z, c = self.me
        for d in (1, 3, 2):
            there = wrap(z + 4 - d)
            self.copy(d - 1, there, c, (x, y, wrap(z + d), c)).wait_recv()
            self.copy(3 + d, there, c, (x, y, z, 1 - c)).start()

    def finish(self):
        x, y, z, c = self.me
        for d in range(4):
            self.copy(3 + d, wrap(z + 4 - d), 1 - c, (x, y, z, 1 - c)).wait_recv()

    def drain(self):
        x, y, z, c = self.me
        for k in range(7):
            self.copy(k, z, c, (x, y, z, 1 - c)).wait_send()


class ExpertGather:
    def __init__(self, me, ref, out, arrive):
        self.me, self.ref, self.out, self.arrive = me, ref, out, arrive

    def upper(self, k, a, b, device):
        part = self.ref.at[a, b, pl.ds(0, HALF)]
        return send(part, part, self.out.at[k], self.arrive.at[k], device)

    def lower(self, k, a, b, device):
        part = self.ref.at[a, b, pl.ds(HALF, HALF)]
        return send(part, part, self.out.at[15 + k], self.arrive.at[15 + k], device)

    def start(self):
        x, y, z, c = self.me
        for d in (1, 3, 2):
            self.upper(d - 1, x, y, (wrap(x + d), y, z, c)).start()
            self.lower(d - 1, x, y, (x, wrap(y + d), z, c)).start()

    def own(self):
        x, y, z, c = self.me
        for d in (1, 3, 2):
            self.upper(3 + d - 1, x, y, (x, wrap(y + d), z, c)).start()
            self.lower(3 + d - 1, x, y, (wrap(x + d), y, z, c)).start()

    def forward(self):
        x, y, z, c = self.me
        for s in (1, 3, 2):
            a, b = wrap(x + 4 - s), wrap(y + 4 - s)
            self.upper(s - 1, a, y, (x, y, z, c)).wait_recv()
            for d in (1, 3, 2):
                self.upper(3 + 3 * s + d - 1, a, y, (x, wrap(y + d), z, c)).start()
            self.lower(s - 1, x, b, (x, y, z, c)).wait_recv()
            for d in (1, 3, 2):
                self.lower(3 + 3 * s + d - 1, x, b, (wrap(x + d), y, z, c)).start()

    def finish(self):
        x, y, z, c = self.me
        for s in range(4):
            for d in (1, 2, 3):
                a, b = wrap(x + 4 - s), wrap(y + 4 - d)
                self.upper(3 + 3 * s + d - 1, a, b, (x, y, z, c)).wait_recv()
                a, b = wrap(x + 4 - d), wrap(y + 4 - s)
                self.lower(3 + 3 * s + d - 1, a, b, (x, y, z, c)).wait_recv()

    def drain(self):
        x, y, z, c = self.me
        for k in range(15):
            self.upper(k, x, y, (x, y, z, c)).wait_send()
            self.lower(k, x, y, (x, y, z, c)).wait_send()


class TensorSum:
    def __init__(self, me, part, near, both, far, out, arrive):
        self.me, self.part, self.near, self.both, self.far = me, part, near, both, far
        self.out, self.arrive = out, arrive

    def to_core(self, i):
        x, y, z, c = self.me
        return send(
            self.part.at[2 * i + 1 - c], self.near.at[i], self.out.at[i], self.arrive.at[i], (x, y, z, 1 - c)
        )

    def along(self, i, k):
        x, y, z, c = self.me
        return send(self.both.at[i], self.far.at[k], self.out.at[4 + k], self.arrive.at[4 + k], (x, y, i, c))

    def paired(self, i):
        x, y, z, c = self.me
        return self.part[2 * i + c].astype(F32) + self.near[i].astype(F32)

    def combine(self, i):
        x, y, z, c = self.me
        self.to_core(i).wait_recv()
        self.both[i] = self.paired(i).astype(BF16)

        @pl.when(z != i)
        def _():
            self.along(i, wrap(i - z + 4) - 1).start()

    def total(self):
        x, y, z, c = self.me
        value = self.paired(z)
        for d in (1, 3, 2):
            self.along(z, d - 1).wait_recv()
            value += self.far[d - 1].astype(F32)
        return value

    def drain(self):
        for i in range(4):
            self.to_core(i).wait_send()
        for k in range(3):
            self.along(0, k).wait_send()


def scaled_inverse(values):
    return lax.rsqrt(jnp.mean(values * values, -1, keepdims=True) + EPS)


def lanes(rows):
    return lax.broadcasted_iota(jnp.int32, (rows, 128), 1)


def partner(values):
    lane = lanes(values.shape[0])
    forth = pltpu.roll(values, 96, 1)
    back = pltpu.roll(values, 32, 1)
    return jnp.where(lax.rem(lane, 64) < 32, forth, back)


def attend_kernel(
    input_ref, cot_ref, routes_ref, gain_attn_ref, gain_moe_ref, w_in_ref, w_out_ref, w_router_ref, cos_ref, sin_ref,
    whole_out, cot_out, query_out, keys_out, values_out, heads_out, lse_out, hidden_ref, mixed_ref, table_ref,
    whole, cot_all, part, near, both, far, pair,
    gather_out, gather_in, cot_send, cot_recv, sum_out, sum_in,
):
    me = place()
    x, y, z, c = me
    rank = z * 2 + c
    greet(z_peers(me) + line_peers(me))
    source = input_ref[...].astype(F32)
    whole[rank] = (source * scaled_inverse(source) * gain_attn_ref[...]).astype(BF16)
    gather = TensorGather(me, lambda k: whole.at[k], gather_out, gather_in)
    gather.start()
    cot_all[x, y] = cot_ref[...]
    cots = ExpertGather(me, cot_all, cot_send, cot_recv)
    cots.start()
    gather.forward()
    gather.finish()

    def project(k, _):
        at = pl.ds(pl.multiple_of(k * ROWS, ROWS), ROWS)
        block = whole[k]
        both_parts = mul(block, w_in_ref[...], NT)
        cosine, sine = cos_ref[at, :], sin_ref[at, :]
        query = both_parts[:, :128]
        query = query * cosine + partner(query) * sine
        query_out[at, :] = (query * 0.125).astype(BF16)
        rest = both_parts[:, 128:]
        low = lanes(ROWS) < HEAD
        rest = jnp.where(low, rest * cosine + partner(rest) * sine, rest)
        first = jnp.where(low, rest, 0.0)
        second = jnp.where(low, 0.0, rest)
        keys_out[0, at, :] = first.astype(BF16)
        keys_out[1, at, :] = pltpu.roll(first, HEAD, 1).astype(BF16)
        values_out[0, at, :] = pltpu.roll(second, HEAD, 1).astype(BF16)
        values_out[1, at, :] = second.astype(BF16)
        return 0

    lax.fori_loop(0, 8, project, 0)
    cots.own()
    cots.forward()
    sums = TensorSum(me, part, near, both, far, sum_out, sum_in)
    for i in range(4):
        count = (i + 1) * 256

        def attend(j, _, i=i, count=count):
            start = i * 256 + j * ROWS
            at = pl.ds(pl.multiple_of(start, ROWS), ROWS)
            query = query_out[at, :]
            row = start + lax.broadcasted_iota(jnp.int32, (ROWS, count), 0)
            allowed = lax.broadcasted_iota(jnp.int32, (ROWS, count), 1) <= row
            result, logs = jnp.zeros((ROWS, 128), F32), []
            for h in (0, 1):
                scores = mul(query, keys_out[h, :count, :], NT)
                scores = jnp.where(allowed, scores, -1e30)
                peak = jnp.max(scores, -1, keepdims=True)
                expo = jnp.exp(scores - peak)
                total = jnp.sum(expo, -1, keepdims=True)
                result += mul(expo.astype(BF16), values_out[h, :count, :]) * (1.0 / total)
                logs.append(peak + jnp.log(total))
            heads_out[at, :] = result.astype(BF16)
            lse_out[at, :] = jnp.where(lanes(ROWS) < HEAD, logs[0], logs[1])
            return 0

        lax.fori_loop(0, 2, attend, 0)

        def outward(j, _, i=i):
            at = pl.ds(pl.multiple_of(i * 256 + j * ROWS, ROWS), ROWS)
            part[2 * i + j] = mul(heads_out[at, :], w_out_ref[...]).astype(BF16)
            return 0

        lax.fori_loop(0, 2, outward, 0)
        sums.to_core(i).start()
        if i > 0:
            sums.combine(i - 1)
    sums.combine(3)
    hidden = source + sums.total()
    hidden_ref[...] = hidden
    mixed = (hidden * scaled_inverse(hidden) * gain_moe_ref[...]).astype(BF16)
    mixed_ref[...] = mixed
    logits = mul(w_router_ref[...], mixed, NT)
    expert = lax.broadcasted_iota(jnp.int32, (32, ROWS), 0)
    named = jnp.zeros((32, ROWS), F32)
    for k in range(8):
        named += jnp.where(routes_ref[k : k + 1, :] == expert, 1.0, 0.0)
    chosen = jnp.where(named > 0, logits, -1e30)
    expo = jnp.where(named > 0, jnp.exp(chosen - jnp.max(chosen, 0, keepdims=True)), 0.0)
    gates = expo / jnp.sum(expo, 0, keepdims=True)
    before = lax.broadcasted_iota(jnp.int32, (ROWS, ROWS), 0) < lax.broadcasted_iota(jnp.int32, (ROWS, ROWS), 1)
    slots = mul(named.astype(BF16), jnp.where(before, 1.0, 0.0).astype(BF16))
    pair[0] = gates
    pair[1] = jnp.where(named > 0, slots, -1.0)
    for g in range(16):
        table_ref[g] = jnp.zeros((8, ROWS), F32)
        table_ref[g, 0:2, :] = pair[0, 2 * g : 2 * g + 2, :]
        table_ref[g, 2:4, :] = pair[1, 2 * g : 2 * g + 2, :]
    cots.finish()

    def keep(k, _):
        whole_out[k] = whole[k]
        return 0

    lax.fori_loop(0, 8, keep, 0)

    def keep_cots(k, _):
        a, b = k // 4, lax.rem(k, 4)
        cot_out[a, b] = cot_all[a, b]
        return 0

    lax.fori_loop(0, 16, keep_cots, 0)
    gather.drain()
    cots.drain()
    sums.drain()


def others():
    return [(d // 4, d % 4) for d in range(1, 16)]


def shifted(me, o):
    x, y, z, c = me
    return wrap(x + o[0]), wrap(y + o[1])


class ExpertSum:
    def __init__(self, me, part, arrived, middle, last, out, arrive):
        self.me, self.part, self.arrived, self.middle, self.last = me, part, arrived, middle, last
        self.out, self.arrive = out, arrive

    def upper(self, d):
        x, y, z, c = self.me
        a = wrap(x + d)
        return send(
            self.part.at[a, :, pl.ds(0, HALF)], self.arrived.at[0, d - 1], self.out.at[d - 1],
            self.arrive.at[d - 1], (a, y, z, c),
        )

    def lower(self, d, j):
        x, y, z, c = self.me
        a, b = wrap(x + 1 + j), wrap(y + d)
        k = 3 + (d - 1) * 4 + j
        return send(
            self.part.at[a, b, pl.ds(HALF, HALF)], self.arrived.at[1, d - 1, a], self.out.at[k],
            self.arrive.at[k], (x, b, z, c),
        )

    def second(self, half, d):
        x, y, z, c = self.me
        k = 15 + half * 3 + d - 1
        device = (x, wrap(y + d), z, c) if half == 0 else (wrap(x + d), y, z, c)
        return send(
            self.middle.at[half, d - 1], self.last.at[half, d - 1], self.out.at[k], self.arrive.at[k], device
        )

    def turn(self, half):
        x, y, z, c = self.me
        for d in (1, 3, 2):
            if half == 0:
                self.upper(d).wait_recv()
            else:
                for j in range(4):
                    self.lower(d, j).wait_recv()
        for d in (1, 3, 2):
            self.middle[half, d - 1] = self.line(half, d).astype(BF16)
            self.second(half, d).start()

    def line(self, half, d):
        x, y, z, c = self.me
        if half == 0:
            b = wrap(y + d)
            value = self.part[x, b, pl.ds(0, HALF), :].astype(F32)
        else:
            b = wrap(x + d)
            value = self.part[b, y, pl.ds(HALF, HALF), :].astype(F32)
        for k in range(3):
            value += self.arrived[half, k, b].astype(F32)
        return value

    def total(self, half):
        value = self.line(half, 0)
        for d in (1, 3, 2):
            self.second(half, d).wait_recv()
            value += self.last[half, d - 1].astype(F32)
        return value

    def drain(self):
        for d in (1, 2, 3):
            self.upper(d).wait_send()
            for j in range(4):
                self.lower(d, j).wait_send()
            self.second(0, d).wait_send()
            self.second(1, d).wait_send()


def experts_kernel(
    mixed_ref, table_ref, cot_ref, shards_ref,
    grads_ref, dmix_ref, dgates_ref, y_ref,
    mixed_all, tables, weights, rows_x, rows_d, rows_g, rows_h, dx, dtab, dback,
    arrived, middle, last, grads, near, both, far,
    mix_out, mix_in, tab_out, tab_in, w_send, w_recv, sum_out, sum_in, dg_out, dg_in, gr_out, gr_in,
):
    me = place()
    x, y, z, c = me
    rank = z * 2 + c
    sides = [(*shifted(me, o), z, c) for o in others()]
    greet(z_peers(me) + sides)
    mixed_all[x, y] = mixed_ref[...]
    gather = ExpertGather(me, mixed_all, mix_out, mix_in)
    gather.start()
    weights[:, rank] = shards_ref[...]
    loads = TensorGather(me, lambda k: weights.at[:, k], w_send, w_recv)
    loads.start()
    gather.own()

    def table_copy(k, device):
        o = others()[k]
        a, b = shifted(me, o)
        return send(table_ref.at[a * 4 + b], tables.at[x, y], tab_out.at[k], tab_in.at[k], device)

    for k, device in enumerate(sides):
        table_copy(k, device).start()
    tables[x, y] = table_ref[x * 4 + y]
    gather.forward()
    loads.forward()
    gather.finish()
    for k, device in enumerate(sides):
        table_copy(k, device).wait_recv()
    loads.finish()

    sums = ExpertSum(me, dx, arrived, middle, last, sum_out, sum_in)
    slot_at = lax.broadcasted_iota(jnp.int32, (CAP, ROWS), 0).astype(F32)

    def weight(m, e):
        return weights[m * 2 + e].reshape(512, WIDTH)

    def chunk(j, _):
        a = wrap(x + 1 + j)
        base = pl.multiple_of(j * 192, 192)
        at = pl.ds(base, 192)
        picks, gate_rows = [], [[], []]
        for b in range(4):
            block = tables[a, b]
            both_picks = []
            for e in (0, 1):
                pick = jnp.where(slot_at == block[2 + e : 3 + e, :], 1.0, 0.0)
                gate_rows[e].append(jnp.sum(pick * block[e : e + 1, :], -1, keepdims=True))
                both_picks.append(pick)
            pick = jnp.concatenate(both_picks, 0)
            picks.append(pick)
            low = pick.astype(BF16)
            got = mul(low, mixed_all[a, b]).astype(BF16)
            into = pl.ds(pl.multiple_of(base + b * CAP, CAP), CAP)
            rows_x[0, into, :] = got[:CAP]
            rows_x[1, into, :] = got[CAP:]
            got = mul(low, cot_ref[a, b]).astype(BF16)
            rows_d[0, into, :] = got[:CAP]
            rows_d[1, into, :] = got[CAP:]
        dots = []
        for e in (0, 1):
            gate = jnp.concatenate(gate_rows[e], 0)
            first = mul(rows_x[e, at, :], weight(0, e), NT)
            second = mul(rows_x[e, at, :], weight(1, e), NT)
            third = mul(rows_d[e, at, :], weight(2, e), NT)
            sigma = 1.0 / (1.0 + jnp.exp(-first))
            active = first * sigma
            hidden = active * second
            dots.append(jnp.sum(third * hidden, -1, keepdims=True))
            rows_h[e, at, :] = (hidden * gate).astype(BF16)
            third = third * gate
            slope = sigma * (1.0 + first * (1.0 - sigma))
            rows_g[e, 0, at, :] = (third * second * slope).astype(BF16)
            rows_g[e, 1, at, :] = (third * active).astype(BF16)
        for b in range(4):
            for e in (0, 1):
                column = dots[e][b * CAP : (b + 1) * CAP]
                dtab[a, b, e : e + 1, :] = jnp.sum(picks[b][e * CAP : (e + 1) * CAP] * column, 0, keepdims=True)
        backs = [
            (mul(rows_g[e, 0, at, :], weight(0, e)) + mul(rows_g[e, 1, at, :], weight(1, e))).astype(BF16)
            for e in (0, 1)
        ]
        for b in range(4):
            span = slice(b * CAP, (b + 1) * CAP)
            both_rows = jnp.concatenate([backs[0][span], backs[1][span]], 0)
            dx[a, b] = mul(picks[b].astype(BF16), both_rows, TN).astype(BF16)

        @pl.when(j < 3)
        def _():
            sums.upper(1 + j).start()

        for d in (1, 3, 2):
            sums.lower(d, j).start()
        ys = [mul(rows_h[e, at, :], weight(2, e)).astype(BF16) for e in (0, 1)]
        for b in range(4):
            span = slice(b * CAP, (b + 1) * CAP)
            both_rows = jnp.concatenate([ys[0][span], ys[1][span]], 0)
            y_ref[a, b] = mul(picks[b].astype(BF16), both_rows, TN).astype(BF16)
        return 0

    for a in range(4):
        for b in range(4):
            dtab[a, b] = jnp.zeros((8, ROWS), F32)
    lax.fori_loop(0, 4, chunk, 0)

    def dgates_copy(k, device):
        a, b = shifted(me, others()[k])
        return send(dtab.at[a, b], dback.at[x, y], dg_out.at[k], dg_in.at[k], device)

    for k, device in enumerate(sides):
        dgates_copy(k, device).start()
    dback[x, y] = dtab[x, y]

    def near_copy(m, i):
        return send(
            grads.at[m, 2 * i + 1 - c], near.at[m, i], gr_out.at[m, i], gr_in.at[m, i], (x, y, z, 1 - c)
        )

    def far_copy(m, i, k):
        return send(both.at[m, i], far.at[m, k], gr_out.at[m, 4 + k], gr_in.at[m, 4 + k], (x, y, i, c))

    def weight_grad(m, _):
        e = lax.rem(m, 2)
        kind = m // 2

        @pl.when(kind < 2)
        def _():
            left = rows_g[e, jnp.minimum(kind, 1)]
            value = mul(left, rows_x[e], TN)
            grads[m] = value.astype(BF16).reshape(8, HALF, WIDTH)

        @pl.when(kind == 2)
        def _():
            value = mul(rows_h[e], rows_d[e], TN)
            grads[m] = value.astype(BF16).reshape(8, HALF, WIDTH)

        for i in range(4):
            near_copy(m, i).start()
        return 0

    def add_core(m, _):
        for i in range(4):
            near_copy(m, i).wait_recv()
            both[m, i] = (grads[m, 2 * i + c].astype(F32) + near[m, i].astype(F32)).astype(BF16)

            @pl.when(z != i)
            def _():
                far_copy(m, i, wrap(i - z + 4) - 1).start()

        return 0

    def grads_total(m, _):
        value = grads[m, 2 * z + c].astype(F32) + near[m, z].astype(F32)
        for d in (1, 3, 2):
            far_copy(m, z, d - 1).wait_recv()
            value += far[m, d - 1].astype(F32)
        grads_ref[m] = value
        return 0

    def weight_grads(m, _):
        weight_grad(m, 0)

        @pl.when(m > 0)
        def _():
            add_core(m - 1, 0)

        return 0

    lax.fori_loop(0, 6, weight_grads, 0)
    add_core(5, 0)
    sums.turn(0)
    sums.turn(1)
    dmix_ref[pl.ds(0, HALF), :] = sums.total(0)
    dmix_ref[pl.ds(HALF, HALF), :] = sums.total(1)
    lax.fori_loop(0, 6, grads_total, 0)
    for k, device in enumerate(sides):
        dgates_copy(k, device).wait_recv()
    dgates_ref[...] = dback[...]

    gather.drain()
    loads.drain()
    sums.drain()
    for k, device in enumerate(sides):
        table_copy(k, device).wait_send()
        dgates_copy(k, device).wait_send()
    for m in range(6):
        for i in range(4):
            near_copy(m, i).wait_send()
        for k in range(3):
            far_copy(m, 0, k).wait_send()


def tensor_others():
    return [(d // 2, d % 2) for d in range(1, 8)]


class ExpertTotal:
    def __init__(self, me, rows, value, arrived, mine, whole, out, arrive):
        self.me, self.rows, self.value, self.arrived = me, rows, value, arrived
        self.mine, self.whole, self.out, self.arrive = mine, whole, out, arrive

    def at(self, g):
        return (
            pl.ds(pl.multiple_of((g // 2) * self.rows, self.rows), self.rows),
            pl.ds(pl.multiple_of(lax.rem(g, 2) * 512, 512), 512),
        )

    def first(self, k):
        x, y, z, c = self.me
        a, b = shifted(self.me, others()[k])
        r, s = self.at(a * 4 + b)
        return send(self.value.at[r, s], self.arrived.at[k], self.out.at[k], self.arrive.at[k], (a, b, z, c))

    def second(self, k):
        x, y, z, c = self.me
        a, b = shifted(self.me, others()[k])
        r, s = self.at(x * 4 + y)
        return send(self.mine, self.whole.at[r, s], self.out.at[15 + k], self.arrive.at[15 + k], (a, b, z, c))

    def start(self):
        for k in range(15):
            self.first(k).start()

    def turn(self):
        x, y, z, c = self.me
        r, s = self.at(x * 4 + y)
        value = self.value[r, s].astype(F32)
        for k in range(15):
            self.first(k).wait_recv()
            value += self.arrived[k].astype(F32)
        value = value.astype(BF16)
        self.mine[...] = value
        self.whole[r, s] = value
        for k in range(15):
            self.second(k).start()

    def finish(self):
        for k in range(15):
            self.second(k).wait_recv()

    def drain(self):
        for k in range(15):
            self.first(k).wait_send()
            self.second(k).wait_send()


def norm_back(grad, values, gain):
    inverse = scaled_inverse(values)
    scaled = grad * gain
    normed = values * inverse
    inner = jnp.mean(scaled * normed, -1, keepdims=True)
    return inverse * (scaled - normed * inner), normed


def backward_kernel(
    input_ref, cot_ref, hidden_ref, mixed_ref, table_ref, dgates_ref, dmix_ref, y_ref,
    gain_attn_ref, gain_moe_ref, w_in_ref, w_out_ref, w_router_ref, cos_ref, sin_ref,
    whole_ref, query_ref, keys_ref, values_ref, heads_ref, lse_ref,
    output_ref, dinput_ref, gin_ref, gout_ref, small_ref, gain_ref,
    arrived, middle, last, dall, pair, small, small_near, small_far, small_mine, small_all,
    dheads, dkeys, dvalues, dproj, gout_value, gout_arrived, gout_mine, gout_all,
    gin_value, gin_arrived, gin_mine, gin_all, gain_near, gain_mid, gain_far, part, near, both, far,
    y_out, y_in, ag_out, ag_in, sm_out, sm_in, go_out, go_in, gi_out, gi_in, ga_out, ga_in, rs_out, rs_in,
):
    me = place()
    x, y, z, c = me
    rank = z * 2 + c
    sides = [(*shifted(me, o), z, c) for o in others()]
    mates = [(x, y, wrap(z + o[0]), lax.rem(c + o[1], 2)) for o in tensor_others()]
    greet(mates + sides)
    outs = ExpertSum(me, y_ref, arrived, middle, last, y_out, y_in)
    for d in (1, 3, 2):
        outs.upper(d).start()
        for j in range(4):
            outs.lower(d, j).start()

    for g in range(16):
        pair[0, 2 * g : 2 * g + 2, :] = table_ref[g, 0:2, :]
        pair[1, 2 * g : 2 * g + 2, :] = dgates_ref[g, 0:2, :]
    gates, dgates = pair[0], pair[1]
    dlog = (gates * (dgates - jnp.sum(gates * dgates, 0, keepdims=True))).astype(BF16)
    dmixed = dmix_ref[...] + mul(dlog, w_router_ref[...], TN)
    hidden = hidden_ref[...]
    dhidden, normed = norm_back(dmixed, hidden, gain_moe_ref[...])
    dhidden += cot_ref[...].astype(F32)
    dinput_ref[...] = dhidden
    dall[rank] = dhidden.astype(BF16)
    gather = TensorGather(me, lambda k: dall.at[k], ag_out, ag_in)
    gather.start()
    small[pl.ds(0, 32), :] = mul(dlog, mixed_ref[...])
    small[pl.ds(32, 8), :] = jnp.broadcast_to(jnp.sum(dmixed * normed, 0, keepdims=True), (8, WIDTH))

    def columns(r):
        return pl.ds(pl.multiple_of(r * 128, 128), 128)

    def small_first(k):
        to = mates[k][2] * 2 + mates[k][3]
        return send(small.at[:, columns(to)], small_near.at[k], sm_out.at[k], sm_in.at[k], mates[k])

    def small_second(k):
        return send(small_mine.at[0], small_far.at[k], sm_out.at[7 + k], sm_in.at[7 + k], sides[k])

    def small_third(k):
        return send(
            small_mine.at[1], small_all.at[:, columns(rank)], sm_out.at[22 + k], sm_in.at[22 + k], mates[k]
        )

    for k in range(7):
        small_first(k).start()
    gather.forward()
    gather.finish()

    def dheads_of(k, _):
        at = pl.ds(pl.multiple_of(k * ROWS, ROWS), ROWS)
        dheads[at, :] = mul(dall[k], w_out_ref[...], NT).astype(BF16)
        return 0

    lax.fori_loop(0, 8, dheads_of, 0)
    gout_value[...] = mul(heads_ref[...], dall[...].reshape(SEQ, WIDTH), TN).astype(BF16)
    outer = ExpertTotal(me, 16, gout_value, gout_arrived, gout_mine, gout_all, go_out, go_in)
    outer.start()
    value = small[:, columns(rank)]
    for k in range(7):
        small_first(k).wait_recv()
        value += small_near[k]
    small_mine[0] = value
    for k in range(15):
        small_second(k).start()
    outs.turn(0)
    outs.turn(1)

    for h in (0, 1):
        dkeys[h] = jnp.zeros((SEQ, 128), F32)
        dvalues[h] = jnp.zeros((SEQ, 128), F32)
    for i in range(4):
        count = (i + 1) * 256

        def attend(j, _, i=i, count=count):
            start = i * 256 + j * ROWS
            at = pl.ds(pl.multiple_of(start, ROWS), ROWS)
            query, grad = query_ref[at, :], dheads[at, :]
            product = grad.astype(F32) * heads_ref[at, :].astype(F32)
            low = lanes(ROWS) < HEAD
            row = start + lax.broadcasted_iota(jnp.int32, (ROWS, count), 0)
            allowed = lax.broadcasted_iota(jnp.int32, (ROWS, count), 1) <= row
            dquery = jnp.zeros((ROWS, 128), F32)
            for h in (0, 1):
                mine = low if h == 0 else jnp.logical_not(low)
                inner = jnp.sum(jnp.where(mine, product, 0.0), -1, keepdims=True)
                scores = mul(query, keys_ref[h, :count, :], NT)
                lse = lse_ref[at, h * HEAD : h * HEAD + 1]
                probs = jnp.where(allowed, jnp.exp(jnp.where(allowed, scores - lse, -1e30)), 0.0)
                dprobs = mul(grad, values_ref[h, :count, :], NT)
                dscores = (probs * (dprobs - inner)).astype(BF16)
                dquery += mul(dscores, keys_ref[h, :count, :])
                dkeys[h, :count, :] += mul(dscores, query, TN)
                dvalues[h, :count, :] += mul(probs.astype(BF16), grad, TN)
            dquery = dquery * 0.125
            dquery = dquery * cos_ref[at, :] - partner(dquery) * sin_ref[at, :]
            dproj[at, :128] = dquery.astype(BF16)
            return 0

        lax.fori_loop(0, 2, attend, 0)

    def undo(k, _):
        at = pl.ds(pl.multiple_of(k * ROWS, ROWS), ROWS)
        low = lanes(ROWS) < HEAD
        dkey = dkeys[0, at, :] + pltpu.roll(dkeys[1, at, :], HEAD, 1)
        dkey = jnp.where(low, dkey, 0.0)
        dkey = dkey * cos_ref[at, :] - partner(dkey) * sin_ref[at, :]
        dvalue = pltpu.roll(dvalues[0, at, :], HEAD, 1) + dvalues[1, at, :]
        dproj[at, 128:] = jnp.where(low, dkey, dvalue).astype(BF16)
        return 0

    lax.fori_loop(0, 8, undo, 0)

    sums = TensorSum(me, part, near, both, far, rs_out, rs_in)
    for i in range(4):

        def outward(j, _, i=i):
            at = pl.ds(pl.multiple_of(i * 256 + j * ROWS, ROWS), ROWS)
            part[2 * i + j] = mul(dproj[at, :], w_in_ref[...]).astype(BF16)
            return 0

        lax.fori_loop(0, 2, outward, 0)
        sums.to_core(i).start()
        if i > 0:
            sums.combine(i - 1)
    sums.combine(3)

    local = mul(dproj[...], whole_ref[...].reshape(SEQ, WIDTH), TN)
    gin_value[...] = local.astype(BF16)
    inner = ExpertTotal(me, 32, gin_value, gin_arrived, gin_mine, gin_all, gi_out, gi_in)
    inner.start()
    gain_mid[0] = jnp.broadcast_to(
        jnp.sum(local * w_in_ref[...].astype(F32), 0, keepdims=True) / gain_attn_ref[...], (8, WIDTH)
    )

    def gain_first(k):
        return send(gain_mid.at[0], gain_near.at[k], ga_out.at[k], ga_in.at[k], mates[k])

    def gain_second(k):
        return send(gain_mid.at[1], gain_far.at[k], ga_out.at[7 + k], ga_in.at[7 + k], sides[k])

    for k in range(7):
        gain_first(k).start()

    value = small_mine[0]
    for k in range(15):
        small_second(k).wait_recv()
        value += small_far[k]
    small_mine[1] = value
    small_all[:, columns(rank)] = value
    for k in range(7):
        small_third(k).start()

    outer.turn()
    for half in (0, 1):
        rows = pl.ds(half * HALF, HALF)
        output_ref[rows, :] = (hidden_ref[rows, :] + outs.total(half)).astype(BF16)

    value = gain_mid[0]
    for k in range(7):
        gain_first(k).wait_recv()
        value += gain_near[k]
    gain_mid[1] = value
    for k in range(15):
        gain_second(k).start()
    inner.turn()

    dnormed = sums.total()
    source = input_ref[...].astype(F32)
    dsource, _ = norm_back(dnormed, source, gain_attn_ref[...])
    dinput_ref[...] += dsource

    for k in range(7):
        small_third(k).wait_recv()
    small_ref[...] = small_all[...]
    outer.finish()
    gout_ref[...] = gout_all[...].astype(F32)
    value = gain_mid[1]
    for k in range(15):
        gain_second(k).wait_recv()
        value += gain_far[k]
    gain_ref[...] = value
    inner.finish()
    gin_ref[...] = gin_all[...].astype(F32)

    gather.drain()
    outs.drain()
    sums.drain()
    outer.drain()
    inner.drain()
    for k in range(7):
        small_first(k).wait_send()
        small_third(k).wait_send()
        gain_first(k).wait_send()
    for k in range(15):
        small_second(k).wait_send()
        gain_second(k).wait_send()


def call(body, inputs, outputs, scratch, number):
    semaphores = [pltpu.SemaphoreType.DMA(s) if isinstance(s, tuple) else s for s in scratch]
    return pl.pallas_call(
        body,
        out_shape=[jax.ShapeDtypeStruct(s, t) for s, t in outputs],
        in_specs=[pl.BlockSpec(memory_space=pltpu.VMEM)] * len(inputs),
        out_specs=[pl.BlockSpec(memory_space=pltpu.VMEM)] * len(outputs),
        scratch_shapes=semaphores,
        compiler_params=pltpu.CompilerParams(
            collective_id=number, has_side_effects=True, vmem_limit_bytes=60 * 1024 * 1024
        ),
    )(*inputs)


def rope_tables():
    half = HEAD // 2
    freqs = np.float32(THETA) ** (-np.arange(half, dtype=np.float32) * np.float32(2.0 / HEAD))
    angles = np.arange(SEQ, dtype=np.float32)[:, None] * freqs[None, :].astype(np.float32)
    cosine, sine = np.cos(angles).astype(np.float32), np.sin(angles).astype(np.float32)
    return np.concatenate([cosine] * 4, 1), np.concatenate([-sine, sine, -sine, sine], 1)


def per_device(
    layer_input, routes, cotangent, gain_attn, gain_moe, w_query, w_key, w_value, w_out, w_router, w_gate, w_up, w_down
):
    vmem = pltpu.VMEM
    gain_attn, gain_moe = gain_attn[None, :], gain_moe[None, :]
    w_in = jnp.concatenate([w_query.T, w_key.T, w_value.T], 0)
    router = w_router.T
    cosine, sine = (jnp.asarray(t) for t in rope_tables())
    block, seq = (ROWS, WIDTH), (8, ROWS, WIDTH)
    every = (4, 4, ROWS, WIDTH)
    whole, cots, query, keys, values, heads, lse, hidden, mixed, table = call(
        attend_kernel,
        (layer_input, cotangent, routes.T, gain_attn, gain_moe, w_in, w_out, router, cosine, sine),
        (
            (seq, BF16), (every, BF16), ((SEQ, 128), BF16), ((2, SEQ, 128), BF16), ((2, SEQ, 128), BF16),
            ((SEQ, 128), BF16), ((SEQ, 128), F32), (block, F32), (block, BF16), ((16, 8, ROWS), F32),
        ),
        (
            vmem(seq, BF16), vmem(every, BF16), vmem(seq, BF16), vmem((4, *block), BF16), vmem((4, *block), BF16),
            vmem((3, *block), BF16), vmem((2, 32, ROWS), F32),
            (7,), (7,), (30,), (30,), (7,), (7,),
        ),
        0,
    )
    shards = jnp.concatenate([w_gate.swapaxes(1, 2), w_up.swapaxes(1, 2), w_down], 0)
    strip = (HALF, WIDTH)
    grads, dmix, dgates, outs = call(
        experts_kernel,
        (mixed, table, cots, shards),
        (((6, *strip), F32), (block, F32), ((4, 4, 8, ROWS), F32), (every, BF16)),
        (
            vmem(every, BF16), vmem((4, 4, 8, ROWS), F32), vmem((6, 8, *strip), BF16),
            vmem((2, 768, WIDTH), BF16), vmem((2, 768, WIDTH), BF16), vmem((2, 2, 768, 512), BF16),
            vmem((2, 768, 512), BF16), vmem(every, BF16), vmem((4, 4, 8, ROWS), F32), vmem((4, 4, 8, ROWS), F32),
            vmem((2, 3, 4, *strip), BF16), vmem((2, 3, *strip), BF16), vmem((2, 3, *strip), BF16),
            vmem((6, 8, *strip), BF16), vmem((6, 4, *strip), BF16), vmem((6, 4, *strip), BF16),
            vmem((6, 3, *strip), BF16),
            (30,), (30,), (15,), (15,), (7,), (7,), (21,), (21,), (15,), (15,), (6, 7), (6, 7),
        ),
        1,
    )
    output, dinput, gin, gout, small, gain = call(
        backward_kernel,
        (
            layer_input, cotangent, hidden, mixed, table, dgates.reshape(16, 8, ROWS), dmix, outs,
            gain_attn, gain_moe, w_in, w_out, router, cosine, sine, whole, query, keys, values, heads, lse,
        ),
        ((block, BF16), (block, F32), ((256, WIDTH), F32), (block, F32), ((40, WIDTH), F32), ((8, WIDTH), F32)),
        (
            vmem((2, 3, 4, *strip), BF16), vmem((2, 3, *strip), BF16), vmem((2, 3, *strip), BF16), vmem(seq, BF16),
            vmem((2, 32, ROWS), F32), vmem((40, WIDTH), F32), vmem((7, 40, 128), F32), vmem((15, 40, 128), F32),
            vmem((2, 40, 128), F32), vmem((40, WIDTH), F32),
            vmem((SEQ, 128), BF16), vmem((2, SEQ, 128), F32), vmem((2, SEQ, 128), F32), vmem((SEQ, 256), BF16),
            vmem(block, BF16), vmem((15, 16, 512), BF16), vmem((16, 512), BF16), vmem(block, BF16),
            vmem((256, WIDTH), BF16), vmem((15, 32, 512), BF16), vmem((32, 512), BF16), vmem((256, WIDTH), BF16),
            vmem((7, 8, WIDTH), F32), vmem((2, 8, WIDTH), F32), vmem((15, 8, WIDTH), F32),
            vmem(seq, BF16), vmem((4, *block), BF16), vmem((4, *block), BF16), vmem((3, *block), BF16),
            (21,), (21,), (7,), (7,), (29,), (29,), (30,), (30,), (30,), (30,), (22,), (22,), (7,), (7,),
        ),
        2,
    )
    return (
        output,
        dinput,
        gin[:128].T,
        gin[128:192].T,
        gin[192:].T,
        gout,
        gain[0],
        small[32],
        small[:32].T,
        grads[0:2].swapaxes(1, 2),
        grads[2:4].swapaxes(1, 2),
        grads[4:6],
    )


def solution(mesh):
    split = Mesh(mesh.devices.reshape(4, 4, 4, 2), AXES)
    in_specs = (
        P(AXES, None),
        P(AXES, None),
        P(AXES, None),
        P(),
        P(),
        P(None, TENSOR),
        P(None, TENSOR),
        P(None, TENSOR),
        P(TENSOR, None),
        P(),
        P(EXPERT, None, TENSOR),
        P(EXPERT, None, TENSOR),
        P(EXPERT, TENSOR, None),
    )
    out_specs = (
        P(AXES, None),
        P(AXES, None),
        P(None, TENSOR),
        P(None, TENSOR),
        P(None, TENSOR),
        P(TENSOR, None),
        P(),
        P(),
        P(),
        P(EXPERT, None, TENSOR),
        P(EXPERT, None, TENSOR),
        P(EXPERT, TENSOR, None),
    )
    return jax.shard_map(per_device, mesh=split, in_specs=in_specs, out_specs=out_specs, check_vma=False)
```

time: 651 us -> 264 us (0.41); the launches traced: 642 us -> 262 us
  Pallas kernels: 0 us -> 245 us
  waiting for transfers between devices: 179 us -> 0 us
  local copies, waits for them, and re-layouts: 139 us -> 12.9 us
  blocking collectives: 114 us -> 0 us
  matrix products: 75.4 us -> 0 us
  other arithmetic: 60 us -> 3.88 us
  starting transfers between devices: 51 us -> 0 us
  between operations: 16.1 us -> 0.7 us
  loops' own time: 6.68 us -> 0 us
    pallas_call x0 -> x3, Pallas kernels: none -> 245 us  [call(): pl.pallas_call(body, out_shape=[jax.ShapeDtypeStruct(s, t) for s, t in ou...]
    all_to_all x6 -> x0, blocking collectives: 114 us -> none  [the longest x2 86.7 us: to_owners(): return lax.all_to_all(rows, EXPERT, split_axis=0, concat_axis=0, tiled=True)]
    all_to_all x8 -> x0, waiting for transfers between devices: 113 us -> none  [the longest x1 32.6 us: per_device(): lax.all_to_all(result, EXPERT, split_axis=0, concat_axis=0, tiled=True)]
    dot_general x36 -> x0, matrix products: 75.4 us -> none  [the longest x2 6 us: one(): jnp.einsum('ngqk,qngd->knd', probs.astype(jnp.bfloat16), d_block, preferr...]
    all_to_all x8 -> x0, starting transfers between devices: 50.4 us -> none  [the longest x3 23.1 us: copy_for_each(): return lax.all_to_all(copies, axis, split_axis=0, concat_axis=0, tiled=True)]
    psum x1 -> x0, waiting for transfers between devices: 44.8 us -> none  [per_device(): lax.psum(grad_w_in[:, :q_width].astype(jnp.bfloat16), EXPERT)]
    reshape x12 -> x0, local copies, waits for them, and re-layouts: 23.1 us -> none  [the longest x2 6.73 us: gather_turned(): b.reshape(-1, *t.shape[1:])]
    reduce_scatter x1 -> x0, waiting for transfers between devices: 21.7 us -> none  [per_device(): lax.psum_scatter(down_full.astype(jnp.bfloat16), TENSOR, scatter_dimensio...]
  transfers between devices with their start and end apart: 12 -> 0, of which waited for: 9 -> 0; matrix products, arithmetic and copies ran while one was open for 20% -> 0% of each run, Pallas kernels for 0% -> 0%
where the time goes in v1:
time: 264 us; the launch traced here: 262 us
  Pallas kernels  245 us (93%)
  local copies, waits for them, and re-layouts  12.9 us (5%)
  other arithmetic  3.88 us (1%)
    pallas_call x3, Pallas kernels, call(): pl.pallas_call(body, out_shape=[jax.ShapeDtypeStruct(s, t) for s, t in ou...  245 us

profile of v1, /device:TPU:1, one launch (start us, length us, event | category | flops | bytes accessed | tf_op | source)
XLA Modules:
  0.0 262.5 jit_solution(16736976681000804124)
XLA Ops:
  0.6 1.1 copy.27
  1.7 1.8 pad_maximum_fusion.1.w_in_ref
  3.5 2.1 pad_maximum_fusion.shards_ref
  5.6 57.4 %shard_map.238 = (bf16[8,128,1024]{2,1,0:T(8,128)(2,1)}, bf16[4,4,128,1024]{3,2,1,0:T(8,128)(2,1)}, bf16[1024,128]{1,0:T(8,128)(2,1)}, bf16[2,1024,128]{2,1,0:T(...) custom-call(bf16[128,1024]{1,0:T(8,128)(2,1)} %input_ref.3, ...), custom_call_target="tpu_custom_call" | custom-call | tf_op jit(solution)/shard_map/pallas_call | solution.py:870
  63.0 107.4 %shard_map.239 = (f32[6,64,1024]{2,1,0:T(8,128)}, f32[128,1024]{1,0:T(8,128)}, f32[4,4,8,128]{3,2,1,0:T(8,128)}, bf16[4,4,128,1024]{3,2,1,0:T(8,128)(2,1)}) custom-call(bf16[128,1024]{1,0:T(8,128)(2,1)} %get-tuple-element.33.mixed_ref, f32[16,8,128]{2,1,0:T(8,128)} %get-tuple-element.34.table_ref, bf16[4,4,128,1024]{3,2,1,0:T(8,128)(2,1)} %get-tuple-element.35.cot_ref, ...), custom_call_target="tpu_custom_call" | custom-call | tf_op jit(solution)/shard_map/pallas_call | solution.py:870
  170.3 80.3 %shard_map.240 = (bf16[128,1024]{1,0:T(8,128)(2,1)}, f32[128,1024]{1,0:T(8,128)}, f32[256,1024]{1,0:T(8,128)}, f32[128,1024]{1,0:T(8,128)}, f32[40,1024]{1,0:T(8,128)}, /*index=5*/f32[8,1024]{1,0:T(8,128)}) custom-call(bf16[128,1024]{1,0:T(8,128)(2,1)} %input_ref.3, bf16[128,1024]{1,0:T(8,128)(2,1)} %cot_ref.3, f32[128,1024]{1,0:T(8,128)} %get-tuple-element.32.hidden_ref, ...), custom_call_target="tpu_custom_call" | custom-call | tf_op jit(solution)/shard_map/pallas_call | solution.py:870
  250.7 0.0 copy-start
  250.7 1.5 slice.30
  252.1 1.4 slice.31
  253.5 1.6 slice_bitcast_fusion.5
  255.1 1.1 slice_bitcast_fusion.2
  256.1 1.9 slice_bitcast_fusion.3
  258.0 0.0 copy-start.3
  258.0 1.0 copy.28
  259.0 0.0 copy-done
  259.0 0.0 copy-start.2
  259.0 0.0 copy-start.1
  259.0 1.2 fusion
  260.2 0.0 copy-done.3
  260.2 0.7 copy.32
  260.9 0.0 copy-done.2
  260.9 0.8 copy.33
  261.7 0.0 copy-done.1
  261.7 0.8 copy.34
Async XLA Ops:
  250.7 8.4 %copy-start = (f32[6,64,1024]{2,1,0:T(8,128)S(1)}, f32[6,64,1024]{2,1,0:T(8,128)}, u32[]{:S(2)}) copy-start(f32[6,64,1024]{2,1,0:T(8,128)} %get-tuple-element.51) | copy-start | bytes 4718596
  258.0 2.2 copy-start.3
  259.0 1.9 copy-start.2
  259.0 2.7 %copy-start.1 = (f32[128,1024]{1,0:T(8,128)S(1)}, f32[128,1024]{1,0:T(8,128)}, u32[]{:S(2)}) copy-start(f32[128,1024]{1,0:T(8,128)} %get-tuple-element.86) | copy-start | bytes 1572868

commit v2 on v1

--- a/solution.py
+++ b/solution.py
@@ -63,87 +63,107 @@
     return [(wrap(x + d), y, z, c) for d in (1, 2, 3)] + [(x, wrap(y + d), z, c) for d in (1, 2, 3)]
 
 
+SHIFTS = (0, 3, 1, 2)
+
+
 class TensorGather:
-    def __init__(self, me, slot, out, arrive):
-        self.me, self.slot, self.out, self.arrive = me, slot, out, arrive
-
-    def copy(self, k, source_z, source_c, device):
-        ref = self.slot(source_z * 2 + source_c)
-        return send(ref, ref, self.out.at[k], self.arrive.at[k], device)
+    def __init__(self, me, slot, out, arrive, mine=None):
+        self.me, self.slot, self.out, self.arrive, self.mine = me, slot, out, arrive, mine
+
+    def copy(self, k, source_z, source_c, device, half=None, mine=None):
+        ref = self.slot(source_z * 2 + source_c, half)
+        return send(ref if mine is None else mine, ref, self.out.at[k], self.arrive.at[k], device)
 
     def start(self):
         x, y, z, c = self.me
-        for d in (1, 3, 2):
-            self.copy(d - 1, z, c, (x, y, wrap(z + d), c)).start()
-        self.copy(3, z, c, (x, y, z, 1 - c)).start()
+        for n, d in ((0, 1), (1, 3)):
+            self.copy(n, z, c, (x, y, wrap(z + d), c), mine=self.mine).start()
+        self.copy(4, z, c, (x, y, z, 1 - c), mine=self.mine).start()
 
     def forward(self):
         x, y, z, c = self.me
-        for d in (1, 3, 2):
+        for n, d in ((0, 1), (1, 3)):
             there = wrap(z + 4 - d)
-            self.copy(d - 1, there, c, (x, y, wrap(z + d), c)).wait_recv()
-            self.copy(3 + d, there, c, (x, y, z, 1 - c)).start()
+            self.copy(n, there, c, (x, y, z, 1 - c)).wait_recv()
+            self.copy(2 + n, there, c, (x, y, wrap(z + d), c), half=n).start()
+            self.copy(5 + n, there, c, (x, y, z, 1 - c)).start()
+
+    def opposite(self):
+        x, y, z, c = self.me
+        for n in (0, 1):
+            self.copy(2 + n, wrap(z + 2), c, (x, y, z, 1 - c), half=n).wait_recv()
+        self.copy(7, wrap(z + 2), c, (x, y, z, 1 - c)).start()
 
     def finish(self):
         x, y, z, c = self.me
-        for d in range(4):
-            self.copy(3 + d, wrap(z + 4 - d), 1 - c, (x, y, z, 1 - c)).wait_recv()
+        for k, d in ((4, 0), (5, 1), (6, 3), (7, 2)):
+            self.copy(k, wrap(z + 4 - d), 1 - c, (x, y, z, 1 - c)).wait_recv()
 
     def drain(self):
         x, y, z, c = self.me
-        for k in range(7):
-            self.copy(k, z, c, (x, y, z, 1 - c)).wait_send()
+        for k in range(8):
+            self.copy(k, z, c, (x, y, z, 1 - c), half=k - 2 if k in (2, 3) else None).wait_send()
 
 
 class ExpertGather:
-    def __init__(self, me, ref, out, arrive):
-        self.me, self.ref, self.out, self.arrive = me, ref, out, arrive
-
-    def upper(self, k, a, b, device):
-        part = self.ref.at[a, b, pl.ds(0, HALF)]
-        return send(part, part, self.out.at[k], self.arrive.at[k], device)
-
-    def lower(self, k, a, b, device):
-        part = self.ref.at[a, b, pl.ds(HALF, HALF)]
-        return send(part, part, self.out.at[15 + k], self.arrive.at[15 + k], device)
+    def __init__(self, me, ref, out, arrive, mine=None):
+        self.me, self.ref, self.out, self.arrive, self.mine = me, ref, out, arrive, mine
+
+    def to(self, h, line, d):
+        x, y, z, c = self.me
+        return (wrap(x + d), y, z, c) if (h == 0) == (line == 1) else (x, wrap(y + d), z, c)
+
+    def copy(self, h, k, i, j, part, device):
+        x, y, z, c = self.me
+        a, b = (wrap(x + i), wrap(y + j)) if h == 0 else (wrap(x + j), wrap(y + i))
+        rows = pl.ds(h * HALF, HALF) if part is None else pl.ds(h * HALF + part * 32, 32)
+        ref = self.ref.at[a, b, rows]
+        source = self.mine.at[rows] if self.mine is not None and i == 0 and j == 0 else ref
+        return send(source, ref, self.out.at[h * 20 + k], self.arrive.at[h * 20 + k], device)
 
     def start(self):
-        x, y, z, c = self.me
-        for d in (1, 3, 2):
-            self.upper(d - 1, x, y, (wrap(x + d), y, z, c)).start()
-            self.lower(d - 1, x, y, (x, wrap(y + d), z, c)).start()
+        for n, d in ((0, 1), (1, 3)):
+            for h in (0, 1):
+                self.copy(h, n, 0, 0, None, self.to(h, 1, d)).start()
+
+    def spread(self, h, s):
+        for m, d in ((0, 1), (1, 3)):
+            self.copy(h, 4 + 2 * s + m, SHIFTS[s], 0, None, self.to(h, 2, d)).start()
 
     def own(self):
-        x, y, z, c = self.me
-        for d in (1, 3, 2):
-            self.upper(3 + d - 1, x, y, (x, wrap(y + d), z, c)).start()
-            self.lower(3 + d - 1, x, y, (wrap(x + d), y, z, c)).start()
-
-    def forward(self):
-        x, y, z, c = self.me
-        for s in (1, 3, 2):
-            a, b = wrap(x + 4 - s), wrap(y + 4 - s)
-            self.upper(s - 1, a, y, (x, y, z, c)).wait_recv()
-            for d in (1, 3, 2):
-                self.upper(3 + 3 * s + d - 1, a, y, (x, wrap(y + d), z, c)).start()
-            self.lower(s - 1, x, b, (x, y, z, c)).wait_recv()
-            for d in (1, 3, 2):
-                self.lower(3 + 3 * s + d - 1, x, b, (wrap(x + d), y, z, c)).start()
+        for h in (0, 1):
+            self.spread(h, 0)
+
+    def relay(self):
+        for n, d in ((0, 1), (1, 3)):
+            for h in (0, 1):
+                self.copy(h, n, 4 - d, 0, None, self.to(h, 1, 1)).wait_recv()
+                self.copy(h, 2 + n, 4 - d, 0, n, self.to(h, 1, d)).start()
+                self.spread(h, 1 + n)
+
+    def opposite(self):
+        for h in (0, 1):
+            for n in (0, 1):
+                self.copy(h, 2 + n, 2, 0, n, self.to(h, 1, 1)).wait_recv()
+            self.spread(h, 3)
+
+    def relay_second(self, s):
+        for m, d in ((0, 1), (1, 3)):
+            for h in (0, 1):
+                self.copy(h, 4 + 2 * s + m, SHIFTS[s], 4 - d, None, self.to(h, 1, 1)).wait_recv()
+                self.copy(h, 12 + 2 * s + m, SHIFTS[s], 4 - d, m, self.to(h, 2, d)).start()
 
     def finish(self):
-        x, y, z, c = self.me
         for s in range(4):
-            for d in (1, 2, 3):
-                a, b = wrap(x + 4 - s), wrap(y + 4 - d)
-                self.upper(3 + 3 * s + d - 1, a, b, (x, y, z, c)).wait_recv()
-                a, b = wrap(x + 4 - d), wrap(y + 4 - s)
-                self.lower(3 + 3 * s + d - 1, a, b, (x, y, z, c)).wait_recv()
+            for m in (0, 1):
+                for h in (0, 1):
+                    self.copy(h, 12 + 2 * s + m, SHIFTS[s], 2, m, self.to(h, 1, 1)).wait_recv()
 
     def drain(self):
-        x, y, z, c = self.me
-        for k in range(15):
-            self.upper(k, x, y, (x, y, z, c)).wait_send()
-            self.lower(k, x, y, (x, y, z, c)).wait_send()
+        for k in range(20):
+            part = 0 if k in (2, 3) or k >= 12 else None
+            for h in (0, 1):
+                self.copy(h, k, 0, 0, part, self.to(h, 1, 1)).wait_send()
 
 
 class TensorSum:
@@ -189,6 +209,10 @@
             self.along(0, k).wait_send()
 
 
+def seq_slot(ref):
+    return lambda k, half: ref.at[k] if half is None else ref.at[k, pl.ds(half * HALF, HALF)]
+
+
 def scaled_inverse(values):
     return lax.rsqrt(jnp.mean(values * values, -1, keepdims=True) + EPS)
 
@@ -205,10 +229,10 @@
 
 
 def attend_kernel(
-    input_ref, cot_ref, routes_ref, gain_attn_ref, gain_moe_ref, w_in_ref, w_out_ref, w_router_ref, cos_ref, sin_ref,
-    whole_out, cot_out, query_out, keys_out, values_out, heads_out, lse_out, hidden_ref, mixed_ref, table_ref,
-    whole, cot_all, part, near, both, far, pair,
-    gather_out, gather_in, cot_send, cot_recv, sum_out, sum_in,
+    input_ref, cot_ref, routes_ref, gain_attn_ref, gain_moe_ref, w_in_ref, w_out_ref, w_router_ref, cos_ref, sin_ref, shards_ref,
+    whole_out, cot_out, weights_out, query_out, keys_out, values_out, heads_out, lse_out, hidden_ref, mixed_ref, table_ref,
+    whole, part, near, both, far, pair,
+    gather_out, gather_in, cot_send, cot_recv, w_send, w_recv, sum_out, sum_in, local,
 ):
     me = place()
     x, y, z, c = me
@@ -216,13 +240,26 @@
     greet(z_peers(me) + line_peers(me))
     source = input_ref[...].astype(F32)
     whole[rank] = (source * scaled_inverse(source) * gain_attn_ref[...]).astype(BF16)
-    gather = TensorGather(me, lambda k: whole.at[k], gather_out, gather_in)
+    gather = TensorGather(me, seq_slot(whole), gather_out, gather_in)
     gather.start()
-    cot_all[x, y] = cot_ref[...]
-    cots = ExpertGather(me, cot_all, cot_send, cot_recv)
+    cots = ExpertGather(me, cot_out, cot_send, cot_recv, cot_ref)
     cots.start()
+    keep_cot = pltpu.make_async_copy(cot_ref, cot_out.at[x, y], local.at[0])
+    keep_cot.start()
+    keep_shard = pltpu.make_async_copy(shards_ref, weights_out.at[:, rank], local.at[1])
+    keep_shard.start()
     gather.forward()
+
+    def slot(k, half):
+        return weights_out.at[:, k] if half is None else weights_out.at[pl.ds(2 * half, 2), k]
+
+    loads = TensorGather(me, slot, w_send, w_recv, shards_ref)
+    loads.start()
+    cots.own()
+    gather.opposite()
     gather.finish()
+    keep_whole = pltpu.make_async_copy(whole, whole_out, local.at[2])
+    keep_whole.start()
 
     def project(k, _):
         at = pl.ds(pl.multiple_of(k * ROWS, ROWS), ROWS)
@@ -244,8 +281,7 @@
         return 0
 
     lax.fori_loop(0, 8, project, 0)
-    cots.own()
-    cots.forward()
+    cots.relay()
     sums = TensorSum(me, part, near, both, far, sum_out, sum_in)
     for i in range(4):
         count = (i + 1) * 256
@@ -280,7 +316,16 @@
         sums.to_core(i).start()
         if i > 0:
             sums.combine(i - 1)
+        if i == 1:
+            cots.opposite()
+            cots.relay_second(0)
+        if i == 2:
+            cots.relay_second(1)
+            loads.forward()
     sums.combine(3)
+    cots.relay_second(2)
+    cots.relay_second(3)
+    loads.opposite()
     hidden = source + sums.total()
     hidden_ref[...] = hidden
     mixed = (hidden * scaled_inverse(hidden) * gain_moe_ref[...]).astype(BF16)
@@ -302,21 +347,13 @@
         table_ref[g, 0:2, :] = pair[0, 2 * g : 2 * g + 2, :]
         table_ref[g, 2:4, :] = pair[1, 2 * g : 2 * g + 2, :]
     cots.finish()
-
-    def keep(k, _):
-        whole_out[k] = whole[k]
-        return 0
-
-    lax.fori_loop(0, 8, keep, 0)
-
-    def keep_cots(k, _):
-        a, b = k // 4, lax.rem(k, 4)
-        cot_out[a, b] = cot_all[a, b]
-        return 0
-
-    lax.fori_loop(0, 16, keep_cots, 0)
+    loads.finish()
+    keep_cot.wait()
+    keep_shard.wait()
+    keep_whole.wait()
     gather.drain()
     cots.drain()
+    loads.drain()
     sums.drain()
 
 
@@ -330,7 +367,8 @@
 
 
 class ExpertSum:
-    def __init__(self, me, part, arrived, middle, last, out, arrive):
+    def __init__(self, me, part, arrived, middle, last, out, arrive, own=None):
+        self.own = own
         self.me, self.part, self.arrived, self.middle, self.last = me, part, arrived, middle, last
         self.out, self.arrive = out, arrive
 
@@ -373,11 +411,12 @@
 
     def line(self, half, d):
         x, y, z, c = self.me
-        if half == 0:
-            b = wrap(y + d)
+        b = wrap((y if half == 0 else x) + d)
+        if self.own is not None:
+            value = self.own[half, b].astype(F32)
+        elif half == 0:
             value = self.part[x, b, pl.ds(0, HALF), :].astype(F32)
         else:
-            b = wrap(x + d)
             value = self.part[b, y, pl.ds(HALF, HALF), :].astype(F32)
         for k in range(3):
             value += self.arrived[half, k, b].astype(F32)
@@ -400,11 +439,11 @@
 
 
 def experts_kernel(
-    mixed_ref, table_ref, cot_ref, shards_ref,
-    grads_ref, dmix_ref, dgates_ref, y_ref,
-    mixed_all, tables, weights, rows_x, rows_d, rows_g, rows_h, dx, dtab, dback,
+    mixed_ref, table_ref, cot_in, shards_ref, weights_in,
+    grads_ref, dmix_ref, dgates_ref, y_out, paired_out,
+    y_ref, cot_ref, mixed_all, tables, weights, rows_x, rows_d, rows_g, rows_h, dx, dtab, dback,
     arrived, middle, last, grads, near, both, far,
-    mix_out, mix_in, tab_out, tab_in, w_send, w_recv, sum_out, sum_in, dg_out, dg_in, gr_out, gr_in,
+    mix_out, mix_in, tab_out, tab_in, w_send, w_recv, sum_out, sum_in, dg_out, dg_in, gr_out, gr_in, local,
 ):
     me = place()
     x, y, z, c = me
@@ -414,9 +453,17 @@
     mixed_all[x, y] = mixed_ref[...]
     gather = ExpertGather(me, mixed_all, mix_out, mix_in)
     gather.start()
-    weights[:, rank] = shards_ref[...]
-    loads = TensorGather(me, lambda k: weights.at[:, k], w_send, w_recv)
+    weights[pl.ds(4, 2), rank] = shards_ref[...]
+
+    def down_slot(k, half):
+        return weights.at[pl.ds(4, 2), k] if half is None else weights.at[4 + half, k]
+
+    loads = TensorGather(me, down_slot, w_send, w_recv)
     loads.start()
+    fetch_cots = pltpu.make_async_copy(cot_in, cot_ref, local.at[0])
+    fetch_cots.start()
+    fetch_weights = pltpu.make_async_copy(weights_in, weights.at[pl.ds(0, 4)], local.at[1])
+    fetch_weights.start()
     gather.own()
 
     def table_copy(k, device):
@@ -427,12 +474,20 @@
     for k, device in enumerate(sides):
         table_copy(k, device).start()
     tables[x, y] = table_ref[x * 4 + y]
-    gather.forward()
+    gather.relay()
+    gather.relay_second(0)
     loads.forward()
-    gather.finish()
+    gather.opposite()
+    gather.relay_second(1)
+    gather.relay_second(2)
+    loads.opposite()
+    gather.relay_second(3)
     for k, device in enumerate(sides):
         table_copy(k, device).wait_recv()
     loads.finish()
+    fetch_cots.wait()
+    fetch_weights.wait()
+    gather.finish()
 
     sums = ExpertSum(me, dx, arrived, middle, last, sum_out, sum_in)
     slot_at = lax.broadcasted_iota(jnp.int32, (CAP, ROWS), 0).astype(F32)
@@ -501,6 +556,7 @@
             span = slice(b * CAP, (b + 1) * CAP)
             both_rows = jnp.concatenate([ys[0][span], ys[1][span]], 0)
             y_ref[a, b] = mul(picks[b].astype(BF16), both_rows, TN).astype(BF16)
+        pltpu.make_async_copy(y_ref.at[a], y_out.at[a], local.at[2 + j]).start()
         return 0
 
     for a in range(4):
@@ -548,7 +604,7 @@
             near_copy(m, i).wait_recv()
             both[m, i] = (grads[m, 2 * i + c].astype(F32) + near[m, i].astype(F32)).astype(BF16)
 
-            @pl.when(z != i)
+            @pl.when((z != i) & (m < 3))
             def _():
                 far_copy(m, i, wrap(i - z + 4) - 1).start()
 
@@ -573,11 +629,13 @@
 
     lax.fori_loop(0, 6, weight_grads, 0)
     add_core(5, 0)
+    keep_paired = pltpu.make_async_copy(both.at[pl.ds(3, 3)], paired_out, local.at[6])
+    keep_paired.start()
     sums.turn(0)
     sums.turn(1)
     dmix_ref[pl.ds(0, HALF), :] = sums.total(0)
     dmix_ref[pl.ds(HALF, HALF), :] = sums.total(1)
-    lax.fori_loop(0, 6, grads_total, 0)
+    lax.fori_loop(0, 3, grads_total, 0)
     for k, device in enumerate(sides):
         dgates_copy(k, device).wait_recv()
     dgates_ref[...] = dback[...]
@@ -591,8 +649,13 @@
     for m in range(6):
         for i in range(4):
             near_copy(m, i).wait_send()
-        for k in range(3):
-            far_copy(m, 0, k).wait_send()
+        if m < 3:
+            for k in range(3):
+                far_copy(m, 0, k).wait_send()
+    keep_paired.wait()
+    for j in range(4):
+        a = wrap(x + 1 + j)
+        pltpu.make_async_copy(y_ref.at[a], y_out.at[a], local.at[2 + j]).wait()
 
 
 def tensor_others():
@@ -658,14 +721,15 @@
 
 
 def backward_kernel(
-    input_ref, cot_ref, hidden_ref, mixed_ref, table_ref, dgates_ref, dmix_ref, y_ref,
+    input_ref, cot_ref, hidden_ref, mixed_ref, table_ref, dgates_ref, dmix_ref, y_ref, paired_ref,
     gain_attn_ref, gain_moe_ref, w_in_ref, w_out_ref, w_router_ref, cos_ref, sin_ref,
-    whole_ref, query_ref, keys_ref, values_ref, heads_ref, lse_ref,
-    output_ref, dinput_ref, gin_ref, gout_ref, small_ref, gain_ref,
+    whole_in, query_ref, keys_ref, values_ref, heads_ref, lse_ref,
+    output_ref, dinput_ref, gin_ref, gout_ref, small_ref, gain_ref, grads_ref,
+    whole_ref, y_own, pair_own, pair_far, probs_0, probs_1, probs_2, probs_3,
     arrived, middle, last, dall, pair, small, small_near, small_far, small_mine, small_all,
     dheads, dkeys, dvalues, dproj, gout_value, gout_arrived, gout_mine, gout_all,
     gin_value, gin_arrived, gin_mine, gin_all, gain_near, gain_mid, gain_far, part, near, both, far,
-    y_out, y_in, ag_out, ag_in, sm_out, sm_in, go_out, go_in, gi_out, gi_in, ga_out, ga_in, rs_out, rs_in,
+    y_out, y_in, ag_out, ag_in, sm_out, sm_in, go_out, go_in, gi_out, gi_in, ga_out, ga_in, rs_out, rs_in, pr_out, pr_in, local,
 ):
     me = place()
     x, y, z, c = me
@@ -673,7 +737,15 @@
     sides = [(*shifted(me, o), z, c) for o in others()]
     mates = [(x, y, wrap(z + o[0]), lax.rem(c + o[1], 2)) for o in tensor_others()]
     greet(mates + sides)
-    outs = ExpertSum(me, y_ref, arrived, middle, last, y_out, y_in)
+    outs = ExpertSum(me, y_ref, arrived, middle, last, y_out, y_in, y_own)
+    fetches = [
+        pltpu.make_async_copy(y_ref.at[x, :, pl.ds(0, HALF)], y_own.at[0], local.at[0]),
+        pltpu.make_async_copy(y_ref.at[:, y, pl.ds(HALF, HALF)], y_own.at[1], local.at[1]),
+        pltpu.make_async_copy(whole_in, whole_ref, local.at[2]),
+        pltpu.make_async_copy(paired_ref.at[:, z], pair_own, local.at[3]),
+    ]
+    for fetch in fetches:
+        fetch.start()
     for d in (1, 3, 2):
         outs.upper(d).start()
         for j in range(4):
@@ -690,7 +762,7 @@
     dhidden += cot_ref[...].astype(F32)
     dinput_ref[...] = dhidden
     dall[rank] = dhidden.astype(BF16)
-    gather = TensorGather(me, lambda k: dall.at[k], ag_out, ag_in)
+    gather = TensorGather(me, seq_slot(dall), ag_out, ag_in)
     gather.start()
     small[pl.ds(0, 32), :] = mul(dlog, mixed_ref[...])
     small[pl.ds(32, 8), :] = jnp.broadcast_to(jnp.sum(dmixed * normed, 0, keepdims=True), (8, WIDTH))
@@ -712,8 +784,43 @@
 
     for k in range(7):
         small_first(k).start()
+    probs_of = (probs_0, probs_1, probs_2, probs_3)
+
+    def again(i):
+        count = (i + 1) * 256
+
+        def one(j, _):
+            start = i * 256 + j * ROWS
+            at = pl.ds(pl.multiple_of(start, ROWS), ROWS)
+            query = query_ref[at, :]
+            row = start + lax.broadcasted_iota(jnp.int32, (ROWS, count), 0)
+            allowed = lax.broadcasted_iota(jnp.int32, (ROWS, count), 1) <= row
+            into = pl.ds(pl.multiple_of(j * ROWS, ROWS), ROWS)
+            for h in (0, 1):
+                scores = mul(query, keys_ref[h, :count, :], NT)
+                lse = lse_ref[at, h * HEAD : h * HEAD + 1]
+                probs = jnp.exp(jnp.where(allowed, scores - lse, -1e30))
+                probs_of[i][h, into, :] = probs.astype(BF16)
+            return 0
+
+        lax.fori_loop(0, 2, one, 0)
+
+    again(3)
+    again(2)
     gather.forward()
+
+    def pair_copy(d):
+        i = wrap(z + d)
+        return send(paired_ref.at[:, i], pair_far.at[d - 1], pr_out.at[d - 1], pr_in.at[d - 1], (x, y, i, c))
+
+    for d in (1, 3, 2):
+        pair_copy(d).start()
+    again(1)
+    again(0)
+    gather.opposite()
     gather.finish()
+    for fetch in fetches:
+        fetch.wait()
 
     def dheads_of(k, _):
         at = pl.ds(pl.multiple_of(k * ROWS, ROWS), ROWS)
@@ -731,9 +838,6 @@
     small_mine[0] = value
     for k in range(15):
         small_second(k).start()
-    outs.turn(0)
-    outs.turn(1)
-
     for h in (0, 1):
         dkeys[h] = jnp.zeros((SEQ, 128), F32)
         dvalues[h] = jnp.zeros((SEQ, 128), F32)
@@ -746,26 +850,29 @@
             query, grad = query_ref[at, :], dheads[at, :]
             product = grad.astype(F32) * heads_ref[at, :].astype(F32)
             low = lanes(ROWS) < HEAD
-            row = start + lax.broadcasted_iota(jnp.int32, (ROWS, count), 0)
-            allowed = lax.broadcasted_iota(jnp.int32, (ROWS, count), 1) <= row
+            taken = pl.ds(pl.multiple_of(j * ROWS, ROWS), ROWS)
             dquery = jnp.zeros((ROWS, 128), F32)
             for h in (0, 1):
                 mine = low if h == 0 else jnp.logical_not(low)
                 inner = jnp.sum(jnp.where(mine, product, 0.0), -1, keepdims=True)
-                scores = mul(query, keys_ref[h, :count, :], NT)
-                lse = lse_ref[at, h * HEAD : h * HEAD + 1]
-                probs = jnp.where(allowed, jnp.exp(jnp.where(allowed, scores - lse, -1e30)), 0.0)
+                probs = probs_of[i][h, taken, :]
                 dprobs = mul(grad, values_ref[h, :count, :], NT)
-                dscores = (probs * (dprobs - inner)).astype(BF16)
+                dscores = (probs.astype(F32) * (dprobs - inner)).astype(BF16)
                 dquery += mul(dscores, keys_ref[h, :count, :])
                 dkeys[h, :count, :] += mul(dscores, query, TN)
-                dvalues[h, :count, :] += mul(probs.astype(BF16), grad, TN)
+                dvalues[h, :count, :] += mul(probs, grad, TN)
             dquery = dquery * 0.125
             dquery = dquery * cos_ref[at, :] - partner(dquery) * sin_ref[at, :]
             dproj[at, :128] = dquery.astype(BF16)
             return 0
 
         lax.fori_loop(0, 2, attend, 0)
+        if i == 0:
+            outs.turn(0)
+        if i == 1:
+            outs.turn(1)
+        if i == 2:
+            outer.turn()
 
     def undo(k, _):
         at = pl.ds(pl.multiple_of(k * ROWS, ROWS), ROWS)
@@ -779,6 +886,23 @@
 
     lax.fori_loop(0, 8, undo, 0)
 
+    product = mul(dproj[...], whole_ref[...].reshape(SEQ, WIDTH), TN)
+    gin_value[...] = product.astype(BF16)
+    inner = ExpertTotal(me, 32, gin_value, gin_arrived, gin_mine, gin_all, gi_out, gi_in)
+    inner.start()
+    gain_mid[0] = jnp.broadcast_to(
+        jnp.sum(product * w_in_ref[...].astype(F32), 0, keepdims=True) / gain_attn_ref[...], (8, WIDTH)
+    )
+
+    def gain_first(k):
+        return send(gain_mid.at[0], gain_near.at[k], ga_out.at[k], ga_in.at[k], mates[k])
+
+    def gain_second(k):
+        return send(gain_mid.at[1], gain_far.at[k], ga_out.at[7 + k], ga_in.at[7 + k], sides[k])
+
+    for k in range(7):
+        gain_first(k).start()
+
     sums = TensorSum(me, part, near, both, far, rs_out, rs_in)
     for i in range(4):
 
@@ -792,23 +916,6 @@
         if i > 0:
             sums.combine(i - 1)
     sums.combine(3)
-
-    local = mul(dproj[...], whole_ref[...].reshape(SEQ, WIDTH), TN)
-    gin_value[...] = local.astype(BF16)
-    inner = ExpertTotal(me, 32, gin_value, gin_arrived, gin_mine, gin_all, gi_out, gi_in)
-    inner.start()
-    gain_mid[0] = jnp.broadcast_to(
-        jnp.sum(local * w_in_ref[...].astype(F32), 0, keepdims=True) / gain_attn_ref[...], (8, WIDTH)
-    )
-
-    def gain_first(k):
-        return send(gain_mid.at[0], gain_near.at[k], ga_out.at[k], ga_in.at[k], mates[k])
-
-    def gain_second(k):
-        return send(gain_mid.at[1], gain_far.at[k], ga_out.at[7 + k], ga_in.at[7 + k], sides[k])
-
-    for k in range(7):
-        gain_first(k).start()
 
     value = small_mine[0]
     for k in range(15):
@@ -819,11 +926,6 @@
     for k in range(7):
         small_third(k).start()
 
-    outer.turn()
-    for half in (0, 1):
-        rows = pl.ds(half * HALF, HALF)
-        output_ref[rows, :] = (hidden_ref[rows, :] + outs.total(half)).astype(BF16)
-
     value = gain_mid[0]
     for k in range(7):
         gain_first(k).wait_recv()
@@ -832,6 +934,9 @@
     for k in range(15):
         gain_second(k).start()
     inner.turn()
+    for half in (0, 1):
+        rows = pl.ds(half * HALF, HALF)
+        output_ref[rows, :] = (hidden_ref[rows, :] + outs.total(half)).astype(BF16)
 
     dnormed = sums.total()
     source = input_ref[...].astype(F32)
@@ -841,6 +946,17 @@
     for k in range(7):
         small_third(k).wait_recv()
     small_ref[...] = small_all[...]
+    for d in (1, 3, 2):
+        pair_copy(d).wait_recv()
+
+    def pair_total(m, _):
+        value = pair_own[m].astype(F32)
+        for k in range(3):
+            value += pair_far[k, m].astype(F32)
+        grads_ref[m] = value
+        return 0
+
+    lax.fori_loop(0, 3, pair_total, 0)
     outer.finish()
     gout_ref[...] = gout_all[...].astype(F32)
     value = gain_mid[1]
@@ -851,6 +967,8 @@
     inner.finish()
     gin_ref[...] = gin_all[...].astype(F32)
 
+    for d in (1, 2, 3):
+        pair_copy(d).wait_send()
     gather.drain()
     outs.drain()
     sums.drain()
@@ -865,13 +983,13 @@
         gain_second(k).wait_send()
 
 
-def call(body, inputs, outputs, scratch, number):
+def call(body, inputs, outputs, scratch, number, loose_in=(), loose_out=()):
     semaphores = [pltpu.SemaphoreType.DMA(s) if isinstance(s, tuple) else s for s in scratch]
     return pl.pallas_call(
         body,
         out_shape=[jax.ShapeDtypeStruct(s, t) for s, t in outputs],
-        in_specs=[pl.BlockSpec(memory_space=pltpu.VMEM)] * len(inputs),
-        out_specs=[pl.BlockSpec(memory_space=pltpu.VMEM)] * len(outputs),
+        in_specs=[pl.BlockSpec(memory_space=pl.ANY if k in loose_in else pltpu.VMEM) for k in range(len(inputs))],
+        out_specs=[pl.BlockSpec(memory_space=pl.ANY if k in loose_out else pltpu.VMEM) for k in range(len(outputs))],
         scratch_shapes=semaphores,
         compiler_params=pltpu.CompilerParams(
             collective_id=number, has_side_effects=True, vmem_limit_bytes=60 * 1024 * 1024
@@ -897,45 +1015,56 @@
     cosine, sine = (jnp.asarray(t) for t in rope_tables())
     block, seq = (ROWS, WIDTH), (8, ROWS, WIDTH)
     every = (4, 4, ROWS, WIDTH)
-    whole, cots, query, keys, values, heads, lse, hidden, mixed, table = call(
+    gate_up = jnp.concatenate([w_gate.swapaxes(1, 2), w_up.swapaxes(1, 2)], 0)
+    strip = (HALF, WIDTH)
+    whole, cots, weights, query, keys, values, heads, lse, hidden, mixed, table = call(
         attend_kernel,
-        (layer_input, cotangent, routes.T, gain_attn, gain_moe, w_in, w_out, router, cosine, sine),
+        (layer_input, cotangent, routes.T, gain_attn, gain_moe, w_in, w_out, router, cosine, sine, gate_up),
         (
-            (seq, BF16), (every, BF16), ((SEQ, 128), BF16), ((2, SEQ, 128), BF16), ((2, SEQ, 128), BF16),
-            ((SEQ, 128), BF16), ((SEQ, 128), F32), (block, F32), (block, BF16), ((16, 8, ROWS), F32),
+            (seq, BF16), (every, BF16), ((4, 8, *strip), BF16), ((SEQ, 128), BF16), ((2, SEQ, 128), BF16),
+            ((2, SEQ, 128), BF16), ((SEQ, 128), BF16), ((SEQ, 128), F32), (block, F32), (block, BF16),
+            ((16, 8, ROWS), F32),
         ),
         (
-            vmem(seq, BF16), vmem(every, BF16), vmem(seq, BF16), vmem((4, *block), BF16), vmem((4, *block), BF16),
+            vmem(seq, BF16), vmem(seq, BF16), vmem((4, *block), BF16), vmem((4, *block), BF16),
             vmem((3, *block), BF16), vmem((2, 32, ROWS), F32),
-            (7,), (7,), (30,), (30,), (7,), (7,),
+            (8,), (8,), (40,), (40,), (8,), (8,), (7,), (7,), (3,),
         ),
         0,
+        (10,),
+        (0, 1, 2),
     )
-    shards = jnp.concatenate([w_gate.swapaxes(1, 2), w_up.swapaxes(1, 2), w_down], 0)
-    strip = (HALF, WIDTH)
-    grads, dmix, dgates, outs = call(
+    grads, dmix, dgates, outs, paired = call(
         experts_kernel,
-        (mixed, table, cots, shards),
-        (((6, *strip), F32), (block, F32), ((4, 4, 8, ROWS), F32), (every, BF16)),
+        (mixed, table, cots, w_down, weights),
+        (((3, *strip), F32), (block, F32), ((4, 4, 8, ROWS), F32), (every, BF16), ((3, 4, *strip), BF16)),
         (
-            vmem(every, BF16), vmem((4, 4, 8, ROWS), F32), vmem((6, 8, *strip), BF16),
+            vmem(every, BF16), vmem(every, BF16), vmem(every, BF16), vmem((4, 4, 8, ROWS), F32),
+            vmem((6, 8, *strip), BF16),
             vmem((2, 768, WIDTH), BF16), vmem((2, 768, WIDTH), BF16), vmem((2, 2, 768, 512), BF16),
             vmem((2, 768, 512), BF16), vmem(every, BF16), vmem((4, 4, 8, ROWS), F32), vmem((4, 4, 8, ROWS), F32),
             vmem((2, 3, 4, *strip), BF16), vmem((2, 3, *strip), BF16), vmem((2, 3, *strip), BF16),
             vmem((6, 8, *strip), BF16), vmem((6, 4, *strip), BF16), vmem((6, 4, *strip), BF16),
-            vmem((6, 3, *strip), BF16),
-            (30,), (30,), (15,), (15,), (7,), (7,), (21,), (21,), (15,), (15,), (6, 7), (6, 7),
+            vmem((3, 3, *strip), BF16),
+            (40,), (40,), (15,), (15,), (8,), (8,), (21,), (21,), (15,), (15,), (6, 7), (6, 7), (7,),
         ),
         1,
+        (2, 4),
+        (3, 4),
     )
-    output, dinput, gin, gout, small, gain = call(
+    output, dinput, gin, gout, small, gain, more = call(
         backward_kernel,
         (
-            layer_input, cotangent, hidden, mixed, table, dgates.reshape(16, 8, ROWS), dmix, outs,
+            layer_input, cotangent, hidden, mixed, table, dgates.reshape(16, 8, ROWS), dmix, outs, paired,
             gain_attn, gain_moe, w_in, w_out, router, cosine, sine, whole, query, keys, values, heads, lse,
         ),
-        ((block, BF16), (block, F32), ((256, WIDTH), F32), (block, F32), ((40, WIDTH), F32), ((8, WIDTH), F32)),
         (
+            (block, BF16), (block, F32), ((256, WIDTH), F32), (block, F32), ((40, WIDTH), F32), ((8, WIDTH), F32),
+            ((3, *strip), F32),
+        ),
+        (
+            vmem(seq, BF16), vmem((2, 4, *strip), BF16), vmem((3, *strip), BF16), vmem((3, 3, *strip), BF16),
+            *(vmem((2, 256, (i + 1) * 256), BF16) for i in range(4)),
             vmem((2, 3, 4, *strip), BF16), vmem((2, 3, *strip), BF16), vmem((2, 3, *strip), BF16), vmem(seq, BF16),
             vmem((2, 32, ROWS), F32), vmem((40, WIDTH), F32), vmem((7, 40, 128), F32), vmem((15, 40, 128), F32),
             vmem((2, 40, 128), F32), vmem((40, WIDTH), F32),
@@ -944,9 +1073,11 @@
             vmem((256, WIDTH), BF16), vmem((15, 32, 512), BF16), vmem((32, 512), BF16), vmem((256, WIDTH), BF16),
             vmem((7, 8, WIDTH), F32), vmem((2, 8, WIDTH), F32), vmem((15, 8, WIDTH), F32),
             vmem(seq, BF16), vmem((4, *block), BF16), vmem((4, *block), BF16), vmem((3, *block), BF16),
-            (21,), (21,), (7,), (7,), (29,), (29,), (30,), (30,), (30,), (30,), (22,), (22,), (7,), (7,),
+            (21,), (21,), (8,), (8,), (29,), (29,), (30,), (30,), (30,), (30,), (22,), (22,), (7,), (7,),
+            (3,), (3,), (4,),
         ),
         2,
+        (7, 8, 16),
     )
     return (
         output,
@@ -959,8 +1090,8 @@
         small[32],
         small[:32].T,
         grads[0:2].swapaxes(1, 2),
-        grads[2:4].swapaxes(1, 2),
-        grads[4:6],
+        jnp.stack([grads[2], more[0]]).swapaxes(1, 2),
+        more[1:3],
     )
 
 

time: 264 us -> 227 us (0.86)
  Pallas kernels: 245 us -> 209 us
    pallas_call x3, Pallas kernels: 245 us -> 209 us  [call(): pl.pallas_call(body, out_shape=[jax.ShapeDtypeStruct(s, t) for s, t in ou...]
where the time goes in v2:
time: 227 us
  Pallas kernels  209 us (92%)
  local copies, waits for them, and re-layouts  12.6 us (6%)
  other arithmetic  4.75 us (2%)
    pallas_call x3, Pallas kernels, call(): pl.pallas_call(body, out_shape=[jax.ShapeDtypeStruct(s, t) for s, t in ou...  209 us

profile of v2, /device:TPU:1, one launch (start us, length us, event | category | flops | bytes accessed | tf_op | source)
XLA Modules:
  0.0 227.1 jit_solution(11657378542563727277)
XLA Ops:
  0.6 1.1 copy.27
  1.7 1.8 pad_maximum_fusion.w_in_ref
  3.5 1.9 pad_maximum_fusion.1.shards_ref
  5.4 57.5 %shard_map.238 = (bf16[8,128,1024]{2,1,0:T(8,128)(2,1)}, bf16[4,4,128,1024]{3,2,1,0:T(8,128)(2,1)}, bf16[4,8,64,1024]{3,2,1,0:T(8,128)(2,1)}, bf16[1024,128]{1,0...) custom-call(bf16[128,1024]{1,0:T(8,128)(2,1)} %input_ref.3, ...), custom_call_target="tpu_custom_call" | custom-call | tf_op jit(solution)/shard_map/pallas_call | solution.py:988
  62.9 77.7 %shard_map.239 = (f32[3,64,1024]{2,1,0:T(8,128)}, f32[128,1024]{1,0:T(8,128)}, f32[4,4,8,128]{3,2,1,0:T(8,128)}, bf16[4,4,128,1024]{3,2,1,0:T(8,128)(2,1)}, bf16[3,4,64,1024]{3,2,1,0:T(8,128)(2,1)}) custom-call(bf16[128,1024]{1,0:T(8,128)(2,1)} %get-tuple-element.36.mixed_ref, f32[16,8,128]{2,1,0:T(8,128)} %get-tuple-element.37.table_ref, ...), custom_call_target="tpu_custom_call" | custom-call | tf_op jit(solution)/shard_map/pallas_call | solution.py:988
  140.6 0.0 copy-start.1
  140.6 73.8 %shard_map.240 = (bf16[128,1024]{1,0:T(8,128)(2,1)}, f32[128,1024]{1,0:T(8,128)}, f32[256,1024]{1,0:T(8,128)}, f32[128,1024]{1,0:T(8,128)}, f32[40,1024]{1,0:T(8...) custom-call(bf16[128,1024]{1,0:T(8,128)(2,1)} %input_ref.3, bf16[128,1024]{1,0:T(8,128)(2,1)} %cot_ref.3, ...), custom_call_target="tpu_custom_call" | custom-call | tf_op jit(solution)/shard_map/pallas_call | solution.py:988
  214.5 0.0 copy-start
  214.5 0.0 copy-start.4
  214.5 0.0 copy-start.3
  214.5 1.5 slice.33
  216.0 1.4 slice.34
  217.3 1.6 slice_bitcast_fusion.4
  218.9 1.0 slice.38
  219.9 0.0 copy-start.2
  219.9 1.9 slice.39
  221.8 0.0 copy-done.1
  221.8 1.1 maximum_bitcast_fusion
  222.9 0.0 copy-done
  223.0 0.8 slice_bitcast_fusion.2
  223.8 1.0 copy.28
  224.8 0.0 copy-done.4
  224.8 0.7 copy.32
  225.5 0.0 copy-done.3
  225.5 0.8 copy.33
  226.3 0.0 copy-done.2
  226.3 0.8 copy.34
  (2 shorter events, 0.1 us)
Async XLA Ops:
  140.6 81.2 %copy-start.1 = (f32[3,64,1024]{2,1,0:T(8,128)S(1)}, f32[3,64,1024]{2,1,0:T(8,128)}, u32[]{:S(2)}) copy-start(f32[3,64,1024]{2,1,0:T(8,128)} %get-tuple-element.56) | copy-start | bytes 2359300
  214.5 8.5 %copy-start = (f32[256,1024]{1,0:T(8,128)S(1)}, f32[256,1024]{1,0:T(8,128)}, u32[]{:S(2)}) copy-start(f32[256,1024]{1,0:T(8,128)} %get-tuple-element.52) | copy-start | bytes 3145732
  214.5 10.3 %copy-start.4 = (bf16[128,1024]{1,0:T(8,128)(2,1)S(1)}, bf16[128,1024]{1,0:T(8,128)(2,1)}, u32[]{:S(2)}) copy-start(bf16[128,1024]{1,0:T(8,128)(2,1)} %get-tuple-element.86) | copy-start | bytes 786436
  214.5 11.0 %copy-start.3 = (f32[128,1024]{1,0:T(8,128)S(1)}, f32[128,1024]{1,0:T(8,128)}, u32[]{:S(2)}) copy-start(f32[128,1024]{1,0:T(8,128)} %get-tuple-element.87) | copy-start | bytes 1572868
  219.9 6.4 %copy-start.2 = (f32[128,1024]{1,0:T(8,128)S(1)}, f32[128,1024]{1,0:T(8,128)}, u32[]{:S(2)}) copy-start(f32[128,1024]{1,0:T(8,128)} %get-tuple-element.91) | copy-start | bytes 1572868

commit v3 on v2

--- a/solution.py
+++ b/solution.py
@@ -229,9 +229,10 @@
 
 
 def attend_kernel(
-    input_ref, cot_ref, routes_ref, gain_attn_ref, gain_moe_ref, w_in_ref, w_out_ref, w_router_ref, cos_ref, sin_ref, shards_ref,
-    whole_out, cot_out, weights_out, query_out, keys_out, values_out, heads_out, lse_out, hidden_ref, mixed_ref, table_ref,
-    whole, part, near, both, far, pair,
+    input_ref, cot_ref, routes_ref, gain_attn_ref, gain_moe_ref, w_query_ref, w_key_ref, w_value_ref,
+    w_out_ref, w_router_ref, cos_ref, sin_ref, gate_ref, up_ref,
+    whole_out, cot_out, weights_out, query_out, keys_out, values_out, heads_out, lse_out, hidden_ref, mixed_ref, table_ref, w_in_ref,
+    shards_ref, whole, part, near, both, far, pair,
     gather_out, gather_in, cot_send, cot_recv, w_send, w_recv, sum_out, sum_in, local,
 ):
     me = place()
@@ -244,6 +245,11 @@
     gather.start()
     cots = ExpertGather(me, cot_out, cot_send, cot_recv, cot_ref)
     cots.start()
+    shards_ref[pl.ds(0, 2)] = gate_ref[...]
+    shards_ref[pl.ds(2, 2)] = up_ref[...]
+    w_in_ref[pl.ds(0, 128), :] = w_query_ref[...].T
+    w_in_ref[pl.ds(128, HEAD), :] = w_key_ref[...]
+    w_in_ref[pl.ds(192, HEAD), :] = w_value_ref[...]
     keep_cot = pltpu.make_async_copy(cot_ref, cot_out.at[x, y], local.at[0])
     keep_cot.start()
     keep_shard = pltpu.make_async_copy(shards_ref, weights_out.at[:, rank], local.at[1])
@@ -441,7 +447,7 @@
 def experts_kernel(
     mixed_ref, table_ref, cot_in, shards_ref, weights_in,
     grads_ref, dmix_ref, dgates_ref, y_out, paired_out,
-    y_ref, cot_ref, mixed_all, tables, weights, rows_x, rows_d, rows_g, rows_h, dx, dtab, dback,
+    y_ref, cot_ref, mixed_all, tables, weights, rows_x, rows_d, rows_g, rows_h, thirds, dx, dtab, dback,
     arrived, middle, last, grads, near, both, far,
     mix_out, mix_in, tab_out, tab_in, w_send, w_recv, sum_out, sum_in, dg_out, dg_in, gr_out, gr_in, local,
 ):
@@ -474,26 +480,49 @@
     for k, device in enumerate(sides):
         table_copy(k, device).start()
     tables[x, y] = table_ref[x * 4 + y]
+    slot_at = lax.broadcasted_iota(jnp.int32, (CAP, ROWS), 0).astype(F32)
+
+    def weight(m, e):
+        return weights[m * 2 + e].reshape(512, WIDTH)
+
+    def pick_of(a, b):
+        block = tables[a, b]
+        return jnp.concatenate([jnp.where(slot_at == block[2 + e : 3 + e, :], 1.0, 0.0) for e in (0, 1)], 0)
+
+    def pick_cots(j, _):
+        a = wrap(x + 1 + j)
+        for b in range(4):
+            got = mul(pick_of(a, b).astype(BF16), cot_ref[a, b]).astype(BF16)
+            into = pl.ds(pl.multiple_of(j * 192 + b * CAP, CAP), CAP)
+            rows_d[0, into, :] = got[:CAP]
+            rows_d[1, into, :] = got[CAP:]
+        return 0
+
+    def back_down(j, _):
+        at = pl.ds(pl.multiple_of(j * 192, 192), 192)
+        for e in (0, 1):
+            thirds[e, at, :] = mul(rows_d[e, at, :], weight(2, e), NT)
+        return 0
+
     gather.relay()
+    loads.forward()
     gather.relay_second(0)
-    loads.forward()
     gather.opposite()
+    for k, device in enumerate(sides):
+        table_copy(k, device).wait_recv()
+    fetch_cots.wait()
+    fetch_weights.wait()
     gather.relay_second(1)
+    lax.fori_loop(0, 2, pick_cots, 0)
     gather.relay_second(2)
     loads.opposite()
+    lax.fori_loop(2, 4, pick_cots, 0)
     gather.relay_second(3)
-    for k, device in enumerate(sides):
-        table_copy(k, device).wait_recv()
     loads.finish()
-    fetch_cots.wait()
-    fetch_weights.wait()
+    lax.fori_loop(0, 4, back_down, 0)
     gather.finish()
 
     sums = ExpertSum(me, dx, arrived, middle, last, sum_out, sum_in)
-    slot_at = lax.broadcasted_iota(jnp.int32, (CAP, ROWS), 0).astype(F32)
-
-    def weight(m, e):
-        return weights[m * 2 + e].reshape(512, WIDTH)
 
     def chunk(j, _):
         a = wrap(x + 1 + j)
@@ -514,15 +543,12 @@
             into = pl.ds(pl.multiple_of(base + b * CAP, CAP), CAP)
             rows_x[0, into, :] = got[:CAP]
             rows_x[1, into, :] = got[CAP:]
-            got = mul(low, cot_ref[a, b]).astype(BF16)
-            rows_d[0, into, :] = got[:CAP]
-            rows_d[1, into, :] = got[CAP:]
         dots = []
         for e in (0, 1):
             gate = jnp.concatenate(gate_rows[e], 0)
             first = mul(rows_x[e, at, :], weight(0, e), NT)
             second = mul(rows_x[e, at, :], weight(1, e), NT)
-            third = mul(rows_d[e, at, :], weight(2, e), NT)
+            third = thirds[e, at, :]
             sigma = 1.0 / (1.0 + jnp.exp(-first))
             active = first * sigma
             hidden = active * second
@@ -551,11 +577,16 @@
 
         for d in (1, 3, 2):
             sums.lower(d, j).start()
+        return 0
+
+    def forward_rows(j, _):
+        a = wrap(x + 1 + j)
+        at = pl.ds(pl.multiple_of(j * 192, 192), 192)
         ys = [mul(rows_h[e, at, :], weight(2, e)).astype(BF16) for e in (0, 1)]
         for b in range(4):
             span = slice(b * CAP, (b + 1) * CAP)
             both_rows = jnp.concatenate([ys[0][span], ys[1][span]], 0)
-            y_ref[a, b] = mul(picks[b].astype(BF16), both_rows, TN).astype(BF16)
+            y_ref[a, b] = mul(pick_of(a, b).astype(BF16), both_rows, TN).astype(BF16)
         pltpu.make_async_copy(y_ref.at[a], y_out.at[a], local.at[2 + j]).start()
         return 0
 
@@ -631,8 +662,10 @@
     add_core(5, 0)
     keep_paired = pltpu.make_async_copy(both.at[pl.ds(3, 3)], paired_out, local.at[6])
     keep_paired.start()
+    lax.fori_loop(0, 2, forward_rows, 0)
     sums.turn(0)
     sums.turn(1)
+    lax.fori_loop(2, 4, forward_rows, 0)
     dmix_ref[pl.ds(0, HALF), :] = sums.total(0)
     dmix_ref[pl.ds(HALF, HALF), :] = sums.total(1)
     lax.fori_loop(0, 3, grads_total, 0)
@@ -997,6 +1030,43 @@
     )(*inputs)
 
 
+def finish_kernel(
+    small_ref, gain_ref, gin, grads, more, output_in, dinput_in, gout_in,
+    query_ref, router_ref, gain_attn_ref, gain_moe_ref,
+    key_out, value_out, gate_out, up_out, down_out, output_out, dinput_out, gout_out,
+):
+    query_ref[...] = gin[:128, :].T
+    router_ref[...] = small_ref[:32, :]
+    gain_moe_ref[...] = small_ref[32:33, :]
+    gain_attn_ref[...] = gain_ref[0:1, :]
+    key_out[...] = gin[128:192, :]
+    value_out[...] = gin[192:256, :]
+    gate_out[...] = grads[0:2]
+    up_out[0] = grads[2]
+    up_out[1] = more[0]
+    down_out[...] = more[1:3]
+    output_out[...] = output_in[...]
+    dinput_out[...] = dinput_in[...]
+    gout_out[...] = gout_in[...]
+
+
+def finish(small, gain, gin, grads, more, output, dinput, gout):
+    strip = (HALF, WIDTH)
+    near = pl.BlockSpec(memory_space=pltpu.VMEM)
+    shapes = (
+        ((WIDTH, 128), F32), ((32, WIDTH), F32), ((1, WIDTH), F32), ((1, WIDTH), F32), (strip, F32), (strip, F32),
+        ((2, *strip), F32), ((2, *strip), F32), ((2, *strip), F32), (output.shape, BF16), (dinput.shape, F32),
+        (gout.shape, F32),
+    )
+    return pl.pallas_call(
+        finish_kernel,
+        out_shape=[jax.ShapeDtypeStruct(s, t) for s, t in shapes],
+        in_specs=[near] * 8,
+        out_specs=[near] * len(shapes),
+        compiler_params=pltpu.CompilerParams(vmem_limit_bytes=60 * 1024 * 1024),
+    )(small, gain, gin, grads, more, output, dinput, gout)
+
+
 def rope_tables():
     half = HEAD // 2
     freqs = np.float32(THETA) ** (-np.arange(half, dtype=np.float32) * np.float32(2.0 / HEAD))
@@ -1010,28 +1080,29 @@
 ):
     vmem = pltpu.VMEM
     gain_attn, gain_moe = gain_attn[None, :], gain_moe[None, :]
-    w_in = jnp.concatenate([w_query.T, w_key.T, w_value.T], 0)
     router = w_router.T
     cosine, sine = (jnp.asarray(t) for t in rope_tables())
     block, seq = (ROWS, WIDTH), (8, ROWS, WIDTH)
     every = (4, 4, ROWS, WIDTH)
-    gate_up = jnp.concatenate([w_gate.swapaxes(1, 2), w_up.swapaxes(1, 2)], 0)
     strip = (HALF, WIDTH)
-    whole, cots, weights, query, keys, values, heads, lse, hidden, mixed, table = call(
+    whole, cots, weights, query, keys, values, heads, lse, hidden, mixed, table, w_in = call(
         attend_kernel,
-        (layer_input, cotangent, routes.T, gain_attn, gain_moe, w_in, w_out, router, cosine, sine, gate_up),
+        (
+            layer_input, cotangent, routes.T, gain_attn, gain_moe, w_query, w_key.T, w_value.T, w_out, router,
+            cosine, sine, w_gate.swapaxes(1, 2), w_up.swapaxes(1, 2),
+        ),
         (
             (seq, BF16), (every, BF16), ((4, 8, *strip), BF16), ((SEQ, 128), BF16), ((2, SEQ, 128), BF16),
             ((2, SEQ, 128), BF16), ((SEQ, 128), BF16), ((SEQ, 128), F32), (block, F32), (block, BF16),
-            ((16, 8, ROWS), F32),
+            ((16, 8, ROWS), F32), ((256, WIDTH), BF16),
         ),
         (
-            vmem(seq, BF16), vmem(seq, BF16), vmem((4, *block), BF16), vmem((4, *block), BF16),
+            vmem((4, *strip), BF16), vmem(seq, BF16), vmem(seq, BF16), vmem((4, *block), BF16), vmem((4, *block), BF16),
             vmem((3, *block), BF16), vmem((2, 32, ROWS), F32),
             (8,), (8,), (40,), (40,), (8,), (8,), (7,), (7,), (3,),
         ),
         0,
-        (10,),
+        (),
         (0, 1, 2),
     )
     grads, dmix, dgates, outs, paired = call(
@@ -1042,7 +1113,8 @@
             vmem(every, BF16), vmem(every, BF16), vmem(every, BF16), vmem((4, 4, 8, ROWS), F32),
             vmem((6, 8, *strip), BF16),
             vmem((2, 768, WIDTH), BF16), vmem((2, 768, WIDTH), BF16), vmem((2, 2, 768, 512), BF16),
-            vmem((2, 768, 512), BF16), vmem(every, BF16), vmem((4, 4, 8, ROWS), F32), vmem((4, 4, 8, ROWS), F32),
+            vmem((2, 768, 512), BF16), vmem((2, 768, 512), F32), vmem(every, BF16), vmem((4, 4, 8, ROWS), F32),
+            vmem((4, 4, 8, ROWS), F32),
             vmem((2, 3, 4, *strip), BF16), vmem((2, 3, *strip), BF16), vmem((2, 3, *strip), BF16),
             vmem((6, 8, *strip), BF16), vmem((6, 4, *strip), BF16), vmem((6, 4, *strip), BF16),
             vmem((3, 3, *strip), BF16),
@@ -1079,19 +1151,21 @@
         2,
         (7, 8, 16),
     )
+    (grad_query, grad_router, grad_attn, grad_moe, grad_key, grad_value, grad_gate, grad_up, grad_down, output, dinput,
+     gout) = finish(small, gain, gin, grads, more, output, dinput, gout)
     return (
         output,
         dinput,
-        gin[:128].T,
-        gin[128:192].T,
-        gin[192:].T,
+        grad_query,
+        grad_key.T,
+        grad_value.T,
         gout,
-        gain[0],
-        small[32],
-        small[:32].T,
-        grads[0:2].swapaxes(1, 2),
-        jnp.stack([grads[2], more[0]]).swapaxes(1, 2),
-        more[1:3],
+        grad_attn.reshape(-1),
+        grad_moe.reshape(-1),
+        grad_router.T,
+        grad_gate.swapaxes(1, 2),
+        grad_up.swapaxes(1, 2),
+        grad_down,
     )
 
 

time: 227 us -> 207 us (0.912)
  local copies, waits for them, and re-layouts: 12.6 us -> 0 us
  other arithmetic: 4.75 us -> 0 us
  Pallas kernels: 209 us -> 206 us
    pallas_call x3, Pallas kernels: 209 us -> 202 us  [call(): pl.pallas_call(body, out_shape=[jax.ShapeDtypeStruct(s, t) for s, t in ou...]
    slice x5 -> x0, local copies, waits for them, and re-layouts: 5.76 us -> none  [the longest x1 1.94 us: per_device(): more[1:3]]
    unnamed x15 -> x0, local copies, waits for them, and re-layouts: 4.39 us -> none
    pallas_call x0 -> x1, Pallas kernels: none -> 4.23 us  [finish(): pl.pallas_call(finish_kernel, out_shape=[jax.ShapeDtypeStruct(s, t) for s...]
    concatenate x2 -> x0, other arithmetic: 3.67 us -> none  [the longest x1 1.87 us: per_device(): gate_up = jnp.concatenate([w_gate.swapaxes(1, 2), w_up.swapaxes(1, 2)], 0)]
    transpose x3 -> x0, local copies, waits for them, and re-layouts: 2.44 us -> none  [the longest x1 1.57 us: per_device(): small[:32]]
where the time goes in v3:
time: 207 us
  Pallas kernels  206 us (100%)
    pallas_call x3, Pallas kernels, call(): pl.pallas_call(body, out_shape=[jax.ShapeDtypeStruct(s, t) for s, t in ou...  202 us
    pallas_call x1, Pallas kernels, finish(): pl.pallas_call(finish_kernel, out_shape=[jax.ShapeDtypeStruct(s, t) for s...  4.23 us

profile of v3, /device:TPU:1, one launch (start us, length us, event | category | flops | bytes accessed | tf_op | source)
XLA Modules:
  0.0 206.6 jit_solution(13912802620632348692)
XLA Ops:
  0.6 57.9 %shard_map.238 = (bf16[8,128,1024]{2,1,0:T(8,128)(2,1)}, bf16[4,4,128,1024]{3,2,1,0:T(8,128)(2,1)}, bf16[4,8,64,1024]{3,2,1,0:T(8,128)(2,1)}, bf16[1024,128]{1,0...) custom-call(bf16[128,1024]{1,0:T(8,128)(2,1)} %input_ref.3, ...), custom_call_target="tpu_custom_call" | custom-call | tf_op jit(solution)/shard_map/pallas_call | solution.py:1021
  58.5 72.6 %shard_map.239 = (f32[3,64,1024]{2,1,0:T(8,128)}, f32[128,1024]{1,0:T(8,128)}, f32[4,4,8,128]{3,2,1,0:T(8,128)}, bf16[4,4,128,1024]{3,2,1,0:T(8,128)(2,1)}, bf16[3,4,64,1024]{3,2,1,0:T(8,128)(2,1)}) custom-call(bf16[128,1024]{1,0:T(8,128)(2,1)} %get-tuple-element.49.mixed_ref, f32[16,8,128]{2,1,0:T(8,128)} %get-tuple-element.50.table_ref, ...), custom_call_target="tpu_custom_call" | custom-call | tf_op jit(solution)/shard_map/pallas_call | solution.py:1021
  131.1 71.2 %shard_map.240 = (bf16[128,1024]{1,0:T(8,128)(2,1)}, f32[128,1024]{1,0:T(8,128)}, f32[256,1024]{1,0:T(8,128)}, f32[128,1024]{1,0:T(8,128)}, f32[40,1024]{1,0:T(8...) custom-call(bf16[128,1024]{1,0:T(8,128)(2,1)} %input_ref.3, bf16[128,1024]{1,0:T(8,128)(2,1)} %cot_ref.3, ...), custom_call_target="tpu_custom_call" | custom-call | tf_op jit(solution)/shard_map/pallas_call | solution.py:1021
  202.3 4.2 %shard_map.241 = (f32[1024,128]{1,0:T(8,128)}, f32[32,1024]{1,0:T(8,128)}, f32[1,1024]{1,0:T(1,128)}, f32[1,1024]{1,0:T(1,128)}, f32[64,1024]{1,0:T(8,128)}, /*i...) custom-call(f32[40,1024]{1,0:T(8,128)} %get-tuple-element.64.small_r, ...), custom_call_target="tpu_custom_call" | custom-call | tf_op jit(solution)/shard_map/pallas_call | solution.py:1061
